TPU v7x, 32 devices: a whole 2x2x4 slice. The times are simulated.
32 devices in a mesh: rad: 4 (over x, core), azi: 8 (over z, y).
Axes of the slice: x: 2, y: 2, z: 4, core: 2. Of those that a mesh axis runs over, the one named last changes fastest.
Arguments:
- fields: float32 [3, 8, 32, 1024], P(None, None, 'rad', 'azi'), may hold values from -6 to 6
- viscosity: float32 [32, 1024], P('rad', 'azi'), may hold values from 0.05 to 0.5
- rotation: float32 [32], replicated, may hold values from 0.2 to 2
- shift_blocks: int32 [1, 32], replicated, may hold values from 0 to 15
Outputs:
- fields_out: float32 [3, 8, 32, 1024], P(None, None, 'rad', 'azi')
Inputs may be any that keep to these rules, and one draw needn't show every extreme that they name: `shift_blocks`: shift of radius r after step t, in blocks of 64 azimuth cells.
All inputs are finite; a program needn't handle non-finite values.
Results may differ from a plain program's by a relative error of at most 0.00002.
Values sent between devices are 32-bit elements; how exact they have to be, the bound alone decides.
A program may use at most 64 MiB of HBM per device.

v0:
```python
import jax
import jax.numpy as jnp
from jax import lax
from jax.sharding import PartitionSpec as P

BLOCK = 64


time_step = 0.3


def with_halo(cells, sides, width, closed):
    for axis, dim in sides:
        count = lax.axis_size(axis)
        ends = count if closed else count - 1
        head = lax.slice_in_dim(cells, 0, width, axis=dim)
        tail = lax.slice_in_dim(cells, cells.shape[dim] - width, cells.shape[dim], axis=dim)
        cells = jnp.concatenate(
            [
                lax.ppermute(tail, axis, [(i, (i + 1) % count) for i in range(ends)]),
                cells,
                lax.ppermute(head, axis, [((i + 1) % count, i) for i in range(ends)]),
            ],
            axis=dim,
        )
    return cells


def from_behind(value, axis, steps):
    count = lax.axis_size(axis)
    pairs = [(source, (source + steps) % count) for source in range(count)]
    return lax.ppermute(value, axis, pairs)


def neighbour_rates(centre, north, south, ahead, behind, viscosity, spin):
    above = jnp.concatenate([centre[:, 1:], centre[:, -1:]], axis=1)
    below = jnp.concatenate([centre[:, :1], centre[:, :-1]], axis=1)
    spread = viscosity * (north + south + ahead + behind + above + below - 6.0 * centre)
    radial_grad = 0.5 * (north - south)
    azimuth_grad = 0.5 * (ahead - behind)
    rate_density = spread[0] - radial_grad[1] - azimuth_grad[2]
    rate_radial = spread[1] - radial_grad[0] + 2.0 * spin * centre[2]
    rate_azimuth = spread[2] - azimuth_grad[0] - 0.5 * spin * centre[1]
    return jnp.stack([rate_density, rate_radial, rate_azimuth])


def body(fields, viscosity, rotation, shift_blocks):
    radii = fields.shape[2]
    band = lax.axis_index("rad")
    first_row = band * radii
    own_spin = lax.dynamic_slice_in_dim(rotation, first_row, radii)[:, None]

    def section_rates(state):
        edge_rows = jnp.stack([state[:, :, 0], state[:, :, -1]], axis=2)
        got_rows = with_halo(edge_rows, (("rad", 2),), 1, False)
        edge_cols = jnp.stack([state[..., 0], state[..., -1]], axis=3)
        got_cols = with_halo(edge_cols, (("azi", 3),), 1, True)
        south = jnp.concatenate([got_rows[:, :, 0:1], state[:, :, :-1]], axis=2)
        north = jnp.concatenate([state[:, :, 1:], got_rows[:, :, 3:4]], axis=2)
        behind = jnp.concatenate([got_cols[..., 0:1], state[..., :-1]], axis=3)
        ahead = jnp.concatenate([state[..., 1:], got_cols[..., 3:4]], axis=3)
        return neighbour_rates(state, north, south, ahead, behind, viscosity, own_spin)

    state = fields
    first = state + time_step * section_rates(state)
    second = 0.75 * state + 0.25 * (first + time_step * section_rates(first))
    state = state / 3.0 + 2.0 / 3.0 * (second + time_step * section_rates(second))
    local_shift = lax.dynamic_slice_in_dim(shift_blocks[0], first_row, radii)
    carried = from_behind(state[..., BLOCK:], "azi", 1)
    moved = jnp.concatenate([carried, state[..., :BLOCK]], axis=3)
    chosen = (local_shift % 2 == 1)[None, None, :, None]
    state = jnp.where(chosen, moved, state)
    levels = lax.axis_size("azi").bit_length() - 1
    for level in range(levels):
        distance = 2**level
        moved = from_behind(state, "azi", distance)
        chosen = (local_shift // (2 * distance) % 2 == 1)[None, None, :, None]
        state = jnp.where(chosen, moved, state)
    return state


def solution(mesh):
    return jax.shard_map(
        body,
        mesh=mesh,
        in_specs=(P(None, None, "rad", "azi"), P("rad", "azi"), P(), P()),
        out_specs=P(None, None, "rad", "azi"),
        check_vma=False,
    )
```

profile of v0, /device:TPU:2, one launch (start us, length us, event | category | flops | bytes accessed | tf_op | source)
XLA Modules:
  0.0 71.1 jit_solution(3787782588965744290)
XLA Ops:
  0.0 1.0 %fusion.44 = (f32[3,8,1,128]{3,2,1,0:T(1,128)S(1)}, f32[3,8,1,128]{3,2,1,0:T(1,128)S(1)}) fusion(f32[3,8,8,128]{3,2,1,0:T(8,128)} %param.4), kind=kLoop, calls=%fused_computation.113 | loop fusion | bytes 49152 | tf_op jit(solution)/shard_map/slice | solution.py:54
  1.0 1.9 %collective-permute-start.1 = (f32[3,8,1,128]{3,2,1,0:T(1,128)S(1)}, f32[3,8,1,128]{3,2,1,0:T(1,128)S(1)}, u32[]{:S(2)}, u32[]{:S(2)}) collective-permute-start(f32[3,8,1,128]{3,2,1,0:T(1,128)S(1)} %get-tuple-element.49), channel_id=1, source_target_pairs={{0,8},{8,16},{16,24},{1,9},{9,17},{17,25},{2,10},{10,18},{18,26},{... | collective-permute-start | bytes 36872 | tf_op jit(solution)/shard_map/ppermute | solution.py:20
  2.9 0.0 copy-start
  2.9 3.8 %collective-permute-start = (f32[3,8,1,128]{3,2,1,0:T(1,128)S(1)}, f32[3,8,1,128]{3,2,1,0:T(1,128)S(1)}, u32[]{:S(2)}, u32[]{:S(2)}) collective-permute-start(f32[3,8,1,128]{3,2,1,0:T(1,128)S(1)} %get-tuple-element.48), channel_id=1, source_target_pairs={{8,0},{16,8},{24,16},{9,1},{17,9},{25,17},{10,2},{18,10},{26,18},{... | collective-permute-start | bytes 36872 | tf_op jit(solution)/shard_map/ppermute | solution.py:22
  6.7 1.1 %fusion.48 = (f32[3,8,8,1]{3,2,1,0:T(8,128)S(1)}, f32[3,8,8,1]{3,2,1,0:T(8,128)S(1)}) fusion(f32[3,8,8,128]{3,2,1,0:T(8,128)} %param.4), kind=kLoop, calls=%fused_computation.117 | loop fusion | bytes 3072 | tf_op jit(solution)/shard_map/slice | solution.py:56
  7.8 1.6 %collective-permute-start.3 = (f32[3,8,8,1]{3,2,1,0:T(8,128)S(1)}, f32[3,8,8,1]{3,2,1,0:T(8,128)S(1)}, u32[]{:S(2)}, u32[]{:S(2)}) collective-permute-start(f32[3,8,8,1]{3,2,1,0:T(8,128)S(1)} %get-tuple-element.57), channel_id=1, source_target_pairs={{0,1},{1,2},{2,3},{3,4},{4,5},{5,6},{6,7},{7,0},{8,9},{9,10},{10,1... | collective-permute-start | bytes 2312 | tf_op jit(solution)/shard_map/ppermute | solution.py:20
  9.3 3.2 %collective-permute-start.2 = (f32[3,8,8,1]{3,2,1,0:T(8,128)S(1)}, f32[3,8,8,1]{3,2,1,0:T(8,128)S(1)}, u32[]{:S(2)}, u32[]{:S(2)}) collective-permute-start(f32[3,8,8,1]{3,2,1,0:T(8,128)S(1)} %get-tuple-element.56), channel_id=1, source_target_pairs={{1,0},{2,1},{3,2},{4,3},{5,4},{6,5},{7,6},{0,7},{9,8},{10,9},{11,1... | collective-permute-start | bytes 2312 | tf_op jit(solution)/shard_map/ppermute | solution.py:22
  12.5 0.0 copy-done
  12.6 0.1 fusion.47
  12.7 0.0 copy-start.2
  12.7 0.6 copy-done.2
  13.3 0.1 broadcast_multiply_fusion.1
  13.4 0.0 collective-permute-done.1
  13.4 0.0 collective-permute-done
  13.5 1.7 %collective-permute-done.3 = f32[3,8,8,1]{3,2,1,0:T(8,128)S(1)} collective-permute-done((f32[3,8,8,1]{3,2,1,0:T(8,128)S(1)}, f32[3,8,8,1]{3,2,1,0:T(8,128)S(1)}, u32[]{:S(2)}, u32[]{:S(2)}) %collective-permute-start.3) | collective-permute-done | bytes 800 | tf_op jit(solution)/shard_map/ppermute | solution.py:20
  15.2 0.0 collective-permute-done.2
  15.2 0.0 copy-start.1
  15.2 0.7 copy-done.1
  15.9 0.1 fusion.2
  16.0 0.1 slice_subtract_fusion.10
  16.2 0.1 fusion.41
  16.3 0.1 fusion.42
  16.4 1.9 %collective-permute-start.5 = (f32[3,8,1,128]{3,2,1,0:T(1,128)S(1)}, f32[3,8,1,128]{3,2,1,0:T(1,128)S(1)}, u32[]{:S(2)}, u32[]{:S(2)}) collective-permute-start(f32[3,8,1,128]{3,2,1,0:T(1,128)S(1)} %get-tuple-element.37), channel_id=1, source_target_pairs={{0,8},{8,16},{16,24},{1,9},{9,17},{17,25},{2,10},{10,18},{18,26},{... | collective-permute-start | bytes 36872 | tf_op jit(solution)/shard_map/ppermute | solution.py:20
  18.3 3.6 %collective-permute-start.4 = (f32[3,8,1,128]{3,2,1,0:T(1,128)S(1)}, f32[3,8,1,128]{3,2,1,0:T(1,128)S(1)}, u32[]{:S(2)}, u32[]{:S(2)}) collective-permute-start(f32[3,8,1,128]{3,2,1,0:T(1,128)S(1)} %get-tuple-element.36), channel_id=1, source_target_pairs={{8,0},{16,8},{24,16},{9,1},{17,9},{25,17},{10,2},{18,10},{26,18},{... | collective-permute-start | bytes 36872 | tf_op jit(solution)/shard_map/ppermute | solution.py:22
  21.9 1.3 %collective-permute-start.7 = (f32[3,8,8,1]{3,2,1,0:T(8,128)S(1)}, f32[3,8,8,1]{3,2,1,0:T(8,128)S(1)}, u32[]{:S(2)}, u32[]{:S(2)}) collective-permute-start(f32[3,8,8,1]{3,2,1,0:T(8,128)S(1)} %get-tuple-element.45), channel_id=1, source_target_pairs={{0,1},{1,2},{2,3},{3,4},{4,5},{5,6},{6,7},{7,0},{8,9},{9,10},{10,1... | collective-permute-start | bytes 2312 | tf_op jit(solution)/shard_map/ppermute | solution.py:20
  23.2 3.5 %collective-permute-start.6 = (f32[3,8,8,1]{3,2,1,0:T(8,128)S(1)}, f32[3,8,8,1]{3,2,1,0:T(8,128)S(1)}, u32[]{:S(2)}, u32[]{:S(2)}) collective-permute-start(f32[3,8,8,1]{3,2,1,0:T(8,128)S(1)} %get-tuple-element.44), channel_id=1, source_target_pairs={{1,0},{2,1},{3,2},{4,3},{5,4},{6,5},{7,6},{0,7},{9,8},{10,9},{11,1... | collective-permute-start | bytes 2312 | tf_op jit(solution)/shard_map/ppermute | solution.py:22
  26.8 0.0 collective-permute-done.5
  26.8 0.0 collective-permute-done.4
  26.8 2.6 %collective-permute-done.7 = f32[3,8,8,1]{3,2,1,0:T(8,128)S(1)} collective-permute-done((f32[3,8,8,1]{3,2,1,0:T(8,128)S(1)}, f32[3,8,8,1]{3,2,1,0:T(8,128)S(1)}, u32[]{:S(2)}, u32[]{:S(2)}) %collective-permute-start.7) | collective-permute-done | bytes 800 | tf_op jit(solution)/shard_map/ppermute | solution.py:20
  29.4 0.1 collective-permute-done.6
  29.5 0.1 fusion.6
  29.6 0.1 slice_subtract_fusion.6
  29.8 0.1 fusion.35
  29.9 0.1 fusion.36
  30.0 1.9 %collective-permute-start.9 = (f32[3,8,1,128]{3,2,1,0:T(1,128)S(1)}, f32[3,8,1,128]{3,2,1,0:T(1,128)S(1)}, u32[]{:S(2)}, u32[]{:S(2)}) collective-permute-start(f32[3,8,1,128]{3,2,1,0:T(1,128)S(1)} %get-tuple-element.25), channel_id=1, source_target_pairs={{0,8},{8,16},{16,24},{1,9},{9,17},{17,25},{2,10},{10,18},{18,26},{... | collective-permute-start | bytes 36872 | tf_op jit(solution)/shard_map/ppermute | solution.py:20
  31.9 3.6 %collective-permute-start.8 = (f32[3,8,1,128]{3,2,1,0:T(1,128)S(1)}, f32[3,8,1,128]{3,2,1,0:T(1,128)S(1)}, u32[]{:S(2)}, u32[]{:S(2)}) collective-permute-start(f32[3,8,1,128]{3,2,1,0:T(1,128)S(1)} %get-tuple-element.24), channel_id=1, source_target_pairs={{8,0},{16,8},{24,16},{9,1},{17,9},{25,17},{10,2},{18,10},{26,18},{... | collective-permute-start | bytes 36872 | tf_op jit(solution)/shard_map/ppermute | solution.py:22
  35.6 0.4 collective-permute-start.11
  35.9 4.4 %collective-permute-start.10 = (f32[3,8,8,1]{3,2,1,0:T(8,128)S(1)}, f32[3,8,8,1]{3,2,1,0:T(8,128)S(1)}, u32[]{:S(2)}, u32[]{:S(2)}) collective-permute-start(f32[3,8,8,1]{3,2,1,0:T(8,128)S(1)} %get-tuple-element.32), channel_id=1, source_target_pairs={{1,0},{2,1},{3,2},{4,3},{5,4},{6,5},{7,6},{0,7},{9,8},{10,9},{11,1... | collective-permute-start | bytes 2312 | tf_op jit(solution)/shard_map/ppermute | solution.py:22
  40.3 0.0 collective-permute-done.9
  40.4 0.0 collective-permute-done.8
  40.4 2.5 %collective-permute-done.11 = f32[3,8,8,1]{3,2,1,0:T(8,128)S(1)} collective-permute-done((f32[3,8,8,1]{3,2,1,0:T(8,128)S(1)}, f32[3,8,8,1]{3,2,1,0:T(8,128)S(1)}, u32[]{:S(2)}, u32[]{:S(2)}) %collective-permute-start.11) | collective-permute-done | bytes 800 | tf_op jit(solution)/shard_map/ppermute | solution.py:20
  42.9 0.0 collective-permute-done.10
  42.9 0.1 fusion.12
  43.1 0.1 slice_subtract_fusion.2
  43.2 0.1 fusion.30
  43.3 0.0 copy-start.3
  43.3 0.1 collective-permute-start.12
  43.4 0.6 copy-done.3
  43.9 0.1 fusion.22
  44.0 6.6 %collective-permute-done.12 = f32[3,8,8,64]{3,2,1,0:T(8,128)S(1)} collective-permute-done((f32[3,8,8,64]{3,2,1,0:T(8,128)S(1)}, f32[3,8,8,64]{3,2,1,0:T(8,128)S(1)}, u32[]{:S(2)}, u32[]{:S(2)}) %collective-permute-start.12) | collective-permute-done | bytes 49184 | tf_op jit(solution)/shard_map/ppermute | solution.py:32
  50.7 0.1 maximum_select_fusion
  50.8 0.1 collective-permute-start.13
  50.8 7.3 %collective-permute-done.13 = f32[3,8,8,128]{3,2,1,0:T(8,128)S(1)} collective-permute-done((f32[3,8,8,128]{3,2,1,0:T(8,128)S(1)}, f32[3,8,8,128]{3,2,1,0:T(8,128)S(1)}, u32[]{:S(2)}, u32[]{:S(2)}) %collective-permute-start.13) | collective-permute-done | bytes 98336 | tf_op jit(solution)/shard_map/ppermute | solution.py:32
  58.1 0.1 broadcast_select_fusion
  58.2 0.0 collective-permute-start.14
  58.2 6.5 %collective-permute-done.14 = f32[3,8,8,128]{3,2,1,0:T(8,128)S(1)} collective-permute-done((f32[3,8,8,128]{3,2,1,0:T(8,128)S(1)}, f32[3,8,8,128]{3,2,1,0:T(8,128)S(1)}, u32[]{:S(2)}, u32[]{:S(2)}) %collective-permute-start.14) | collective-permute-done | bytes 98336 | tf_op jit(solution)/shard_map/ppermute | solution.py:32
  64.7 0.1 broadcast_select_fusion.1
  64.8 0.0 collective-permute-start.15
  64.9 5.5 %collective-permute-done.15 = f32[3,8,8,128]{3,2,1,0:T(8,128)S(1)} collective-permute-done((f32[3,8,8,128]{3,2,1,0:T(8,128)S(1)}, f32[3,8,8,128]{3,2,1,0:T(8,128)S(1)}, u32[]{:S(2)}, u32[]{:S(2)}) %collective-permute-start.15) | collective-permute-done | bytes 98336 | tf_op jit(solution)/shard_map/ppermute | solution.py:32
  70.4 0.7 %broadcast_select_fusion.2 = f32[3,8,8,128]{3,2,1,0:T(8,128)} fusion(f32[3,8,8,128]{3,2,1,0:T(8,128)S(1)} %collective-permute-done.15, f32[3,8,8,128]{3,2,1,0:T(8,128)S(1)} %broadcast_select_fusion.1, pred[8]{0:T(512)(128)(4,1)S(1)} %get-tuple-element.58), kind=kLoop, calls=%fused_computation.43 | loop fusion | flops 24576 | bytes 294920 | tf_op jit(solution)/shard_map/jit(_where)/select_n | solution.py:78
  (17 shorter events, 0.4 us)
Async XLA Ops:
  1.0 12.4 %collective-permute-start.1 = (f32[3,8,1,128]{3,2,1,0:T(1,128)S(1)}, f32[3,8,1,128]{3,2,1,0:T(1,128)S(1)}, u32[]{:S(2)}, u32[]{:S(2)}) collective-permute-start(f32[3,8,1,128]{3,2,1,0:T(1,128)S(1)} %get-tuple-element.49), channel_id=1, source_target_pairs={{0,8},{8,16},{16,24},{1,9},{9,17},{17,25},{2,10},{10,18},{18,26},{... | collective-permute-start | bytes 36872 | tf_op jit(solution)/shard_map/ppermute | solution.py:20
  2.9 9.6 %copy-start = (f32[3,8,8,128]{3,2,1,0:T(8,128)S(1)}, f32[3,8,8,128]{3,2,1,0:T(8,128)}, u32[]{:S(2)}) copy-start(f32[3,8,8,128]{3,2,1,0:T(8,128)} %param.4) | copy-start | bytes 294916
  2.9 10.5 %collective-permute-start = (f32[3,8,1,128]{3,2,1,0:T(1,128)S(1)}, f32[3,8,1,128]{3,2,1,0:T(1,128)S(1)}, u32[]{:S(2)}, u32[]{:S(2)}) collective-permute-start(f32[3,8,1,128]{3,2,1,0:T(1,128)S(1)} %get-tuple-element.48), channel_id=1, source_target_pairs={{8,0},{16,8},{24,16},{9,1},{17,9},{25,17},{10,2},{18,10},{26,18},{... | collective-permute-start | bytes 36872 | tf_op jit(solution)/shard_map/ppermute | solution.py:22
  7.8 7.4 %collective-permute-start.3 = (f32[3,8,8,1]{3,2,1,0:T(8,128)S(1)}, f32[3,8,8,1]{3,2,1,0:T(8,128)S(1)}, u32[]{:S(2)}, u32[]{:S(2)}) collective-permute-start(f32[3,8,8,1]{3,2,1,0:T(8,128)S(1)} %get-tuple-element.57), channel_id=1, source_target_pairs={{0,1},{1,2},{2,3},{3,4},{4,5},{5,6},{6,7},{7,0},{8,9},{9,10},{10,1... | collective-permute-start | bytes 2312 | tf_op jit(solution)/shard_map/ppermute | solution.py:20
  9.3 5.8 %collective-permute-start.2 = (f32[3,8,8,1]{3,2,1,0:T(8,128)S(1)}, f32[3,8,8,1]{3,2,1,0:T(8,128)S(1)}, u32[]{:S(2)}, u32[]{:S(2)}) collective-permute-start(f32[3,8,8,1]{3,2,1,0:T(8,128)S(1)} %get-tuple-element.56), channel_id=1, source_target_pairs={{1,0},{2,1},{3,2},{4,3},{5,4},{6,5},{7,6},{0,7},{9,8},{10,9},{11,1... | collective-permute-start | bytes 2312 | tf_op jit(solution)/shard_map/ppermute | solution.py:22
  12.7 0.7 copy-start.2
  15.2 0.7 copy-start.1
  16.4 10.4 %collective-permute-start.5 = (f32[3,8,1,128]{3,2,1,0:T(1,128)S(1)}, f32[3,8,1,128]{3,2,1,0:T(1,128)S(1)}, u32[]{:S(2)}, u32[]{:S(2)}) collective-permute-start(f32[3,8,1,128]{3,2,1,0:T(1,128)S(1)} %get-tuple-element.37), channel_id=1, source_target_pairs={{0,8},{8,16},{16,24},{1,9},{9,17},{17,25},{2,10},{10,18},{18,26},{... | collective-permute-start | bytes 36872 | tf_op jit(solution)/shard_map/ppermute | solution.py:20
  18.3 8.5 %collective-permute-start.4 = (f32[3,8,1,128]{3,2,1,0:T(1,128)S(1)}, f32[3,8,1,128]{3,2,1,0:T(1,128)S(1)}, u32[]{:S(2)}, u32[]{:S(2)}) collective-permute-start(f32[3,8,1,128]{3,2,1,0:T(1,128)S(1)} %get-tuple-element.36), channel_id=1, source_target_pairs={{8,0},{16,8},{24,16},{9,1},{17,9},{25,17},{10,2},{18,10},{26,18},{... | collective-permute-start | bytes 36872 | tf_op jit(solution)/shard_map/ppermute | solution.py:22
  21.9 7.5 %collective-permute-start.7 = (f32[3,8,8,1]{3,2,1,0:T(8,128)S(1)}, f32[3,8,8,1]{3,2,1,0:T(8,128)S(1)}, u32[]{:S(2)}, u32[]{:S(2)}) collective-permute-start(f32[3,8,8,1]{3,2,1,0:T(8,128)S(1)} %get-tuple-element.45), channel_id=1, source_target_pairs={{0,1},{1,2},{2,3},{3,4},{4,5},{5,6},{6,7},{7,0},{8,9},{9,10},{10,1... | collective-permute-start | bytes 2312 | tf_op jit(solution)/shard_map/ppermute | solution.py:20
  23.2 6.3 %collective-permute-start.6 = (f32[3,8,8,1]{3,2,1,0:T(8,128)S(1)}, f32[3,8,8,1]{3,2,1,0:T(8,128)S(1)}, u32[]{:S(2)}, u32[]{:S(2)}) collective-permute-start(f32[3,8,8,1]{3,2,1,0:T(8,128)S(1)} %get-tuple-element.44), channel_id=1, source_target_pairs={{1,0},{2,1},{3,2},{4,3},{5,4},{6,5},{7,6},{0,7},{9,8},{10,9},{11,1... | collective-permute-start | bytes 2312 | tf_op jit(solution)/shard_map/ppermute | solution.py:22
  30.0 10.4 %collective-permute-start.9 = (f32[3,8,1,128]{3,2,1,0:T(1,128)S(1)}, f32[3,8,1,128]{3,2,1,0:T(1,128)S(1)}, u32[]{:S(2)}, u32[]{:S(2)}) collective-permute-start(f32[3,8,1,128]{3,2,1,0:T(1,128)S(1)} %get-tuple-element.25), channel_id=1, source_target_pairs={{0,8},{8,16},{16,24},{1,9},{9,17},{17,25},{2,10},{10,18},{18,26},{... | collective-permute-start | bytes 36872 | tf_op jit(solution)/shard_map/ppermute | solution.py:20
  31.9 8.4 %collective-permute-start.8 = (f32[3,8,1,128]{3,2,1,0:T(1,128)S(1)}, f32[3,8,1,128]{3,2,1,0:T(1,128)S(1)}, u32[]{:S(2)}, u32[]{:S(2)}) collective-permute-start(f32[3,8,1,128]{3,2,1,0:T(1,128)S(1)} %get-tuple-element.24), channel_id=1, source_target_pairs={{8,0},{16,8},{24,16},{9,1},{17,9},{25,17},{10,2},{18,10},{26,18},{... | collective-permute-start | bytes 36872 | tf_op jit(solution)/shard_map/ppermute | solution.py:22
  35.6 7.4 %collective-permute-start.11 = (f32[3,8,8,1]{3,2,1,0:T(8,128)S(1)}, f32[3,8,8,1]{3,2,1,0:T(8,128)S(1)}, u32[]{:S(2)}, u32[]{:S(2)}) collective-permute-start(f32[3,8,8,1]{3,2,1,0:T(8,128)S(1)} %get-tuple-element.33), channel_id=1, source_target_pairs={{0,1},{1,2},{2,3},{3,4},{4,5},{5,6},{6,7},{7,0},{8,9},{9,10},{10,1... | collective-permute-start | bytes 2312 | tf_op jit(solution)/shard_map/ppermute | solution.py:20
  35.9 7.0 %collective-permute-start.10 = (f32[3,8,8,1]{3,2,1,0:T(8,128)S(1)}, f32[3,8,8,1]{3,2,1,0:T(8,128)S(1)}, u32[]{:S(2)}, u32[]{:S(2)}) collective-permute-start(f32[3,8,8,1]{3,2,1,0:T(8,128)S(1)} %get-tuple-element.32), channel_id=1, source_target_pairs={{1,0},{2,1},{3,2},{4,3},{5,4},{6,5},{7,6},{0,7},{9,8},{10,9},{11,1... | collective-permute-start | bytes 2312 | tf_op jit(solution)/shard_map/ppermute | solution.py:22
  43.3 0.7 copy-start.3
  43.3 7.4 %collective-permute-start.12 = (f32[3,8,8,64]{3,2,1,0:T(8,128)S(1)}, f32[3,8,8,64]{3,2,1,0:T(8,128)S(1)}, u32[]{:S(2)}, u32[]{:S(2)}) collective-permute-start(f32[3,8,8,64]{3,2,1,0:T(8,128)S(1)} %get-tuple-element.20), channel_id=1, source_target_pairs={{0,1},{1,2},{2,3},{3,4},{4,5},{5,6},{6,7},{7,0},{8,9},{9,10},{10,1... | collective-permute-start | bytes 147464 | tf_op jit(solution)/shard_map/ppermute | solution.py:32
  50.8 7.4 %collective-permute-start.13 = (f32[3,8,8,128]{3,2,1,0:T(8,128)S(1)}, f32[3,8,8,128]{3,2,1,0:T(8,128)S(1)}, u32[]{:S(2)}, u32[]{:S(2)}) collective-permute-start(f32[3,8,8,128]{3,2,1,0:T(8,128)S(1)} %maximum_select_fusion), channel_id=1, source_target_pairs={{0,1},{1,2},{2,3},{3,4},{4,5},{5,6},{6,7},{7,0},{8,9},{9,10},{10,1... | collective-permute-start | bytes 294920 | tf_op jit(solution)/shard_map/ppermute | solution.py:32
  58.2 6.5 %collective-permute-start.14 = (f32[3,8,8,128]{3,2,1,0:T(8,128)S(1)}, f32[3,8,8,128]{3,2,1,0:T(8,128)S(1)}, u32[]{:S(2)}, u32[]{:S(2)}) collective-permute-start(f32[3,8,8,128]{3,2,1,0:T(8,128)S(1)} %broadcast_select_fusion), channel_id=1, source_target_pairs={{0,2},{1,3},{2,4},{3,5},{4,6},{5,7},{6,0},{7,1},{8,10},{9,11},{10,... | collective-permute-start | bytes 294920 | tf_op jit(solution)/shard_map/ppermute | solution.py:32
  64.8 5.5 %collective-permute-start.15 = (f32[3,8,8,128]{3,2,1,0:T(8,128)S(1)}, f32[3,8,8,128]{3,2,1,0:T(8,128)S(1)}, u32[]{:S(2)}, u32[]{:S(2)}) collective-permute-start(f32[3,8,8,128]{3,2,1,0:T(8,128)S(1)} %broadcast_select_fusion.1), channel_id=1, source_target_pairs={{0,4},{1,5},{2,6},{3,7},{4,0},{5,1},{6,2},{7,3},{8,12},{9,13},{10,... | collective-permute-start | bytes 294920 | tf_op jit(solution)/shard_map/ppermute | solution.py:32
where the time goes:
time: 71.4 us; the launch traced here: 71.1 us
  waiting for transfers between devices  32.8 us (46%)
  starting transfers between devices  31.3 us (44%)
  local copies, waits for them, and re-layouts  4.62 us (6%)
  other arithmetic  2 us (3%)
    ppermute x4, waiting for transfers between devices, from_behind(): return lax.ppermute(value, axis, pairs)  25.9 us
    ppermute x6, starting transfers between devices, with_halo(): lax.ppermute(head, axis, [((i + 1) % count, i) for i in range(ends)])  22.2 us
    ppermute x6, starting transfers between devices, with_halo(): lax.ppermute(tail, axis, [(i, (i + 1) % count) for i in range(ends)])  8.95 us
    ppermute x6, waiting for transfers between devices, with_halo(): lax.ppermute(tail, axis, [(i, (i + 1) % count) for i in range(ends)])  6.83 us
    unnamed x8, local copies, waits for them, and re-layouts  1.93 us
  transfers between devices with their start and end apart: 16, of which 8 were waited for; matrix products, arithmetic and copies ran while one was open for 2% of the time, Pallas kernels for 0%

commit v1 on v0

v1 whole, which is shorter than its diff:
```python
import functools

import jax
import jax.numpy as jnp
from jax import lax
from jax.experimental import pallas as pl
from jax.experimental.pallas import tpu as pltpu
from jax.sharding import PartitionSpec as P

BLOCK = 64
time_step = 0.3
MESH = pl.DeviceIdType.MESH
DEPTH = 3


def neighbour_rates(centre, north, south, viscosity, spin):
    width = centre.shape[-1]
    level = lax.broadcasted_iota(jnp.int32, centre.shape, 1)
    ahead = pltpu.roll(centre, width - 1, axis=2)
    behind = pltpu.roll(centre, 1, axis=2)
    above = jnp.where(level == 7, centre, pltpu.roll(centre, 7, axis=1))
    below = jnp.where(level == 0, centre, pltpu.roll(centre, 1, axis=1))
    spread = viscosity * (north + south + ahead + behind + above + below - 6.0 * centre)
    radial_grad = 0.5 * (north - south)
    azimuth_grad = 0.5 * (ahead - behind)
    rate_density = spread[0] - radial_grad[1] - azimuth_grad[2]
    rate_radial = spread[1] - radial_grad[0] + 2.0 * spin * centre[2]
    rate_azimuth = spread[2] - azimuth_grad[0] - 0.5 * spin * centre[1]
    return jnp.stack([rate_density, rate_radial, rate_azimuth])


def kernel(
    bands, sectors, chunks,
    fields, viscosity, rotation, shifts, out,
    own, side, first, second, final, partner, lines, pack, from_ahead, from_behind,
    halo_sent, halo_got, pair_sent, pair_got, right_sent, right_got, left_sent, left_got,
):
    radii = viscosity.shape[0]
    places = sectors // 2
    band = lax.axis_index("rad")
    sector = lax.axis_index("azi")
    place, parity = sector // 2, sector % 2
    has_up, has_down = band < bands - 1, band > 0

    def at(dr, da):
        return (lax.rem(band + dr + bands, bands), lax.rem(sector + da + sectors, sectors))

    barrier = pltpu.get_barrier_semaphore()
    greeted = [(dr, da) for dr in (-1, 0, 1) for da in (-1, 0, 1) if (dr, da) != (0, 0)] + [(0, -2), (0, 2)]
    for dr, da in greeted:
        pl.semaphore_signal(barrier, inc=1, device_id=at(dr, da), device_id_type=MESH)

    lane = lax.broadcasted_iota(jnp.int32, (8, 128), 1)
    slot = ((lane + 4) // 8) % 16
    for group in range(2):
        packed = None
        for r in range(4 * group, 4 * group + 4):
            for f in range(4):
                if f < 3:
                    tile = fields[f, pl.ds(r, 8, stride=8), :]
                else:
                    tile = jnp.broadcast_to(viscosity[pl.ds(r, 1), :], (8, 128))
                own[DEPTH + r, f] = tile
                index = (r % 4) * 4 + f
                if index == 0:
                    packed = tile
                else:
                    packed = jnp.where(slot == index, pltpu.roll(tile, 8 * index, axis=1), packed)
        pack[group] = packed

    pl.semaphore_wait(barrier, len(greeted))

    def remote(src, dst, sent, got, device):
        return pltpu.make_async_remote_copy(
            src_ref=src, dst_ref=dst, send_sem=sent, recv_sem=got, device_id=device, device_id_type=MESH
        )

    def halo(index, src, dst, device):
        return remote(src, dst, halo_sent.at[index], halo_got.at[index], device)

    last = DEPTH + radii
    up = [
        halo(0, own.at[radii:last], own.at[0:DEPTH], at(1, 0)),
        halo(4, pack.at[1], from_behind.at[0, 1], at(1, 1)),
        halo(5, pack.at[1], from_ahead.at[0, 1], at(1, -1)),
    ]
    down = [
        halo(1, own.at[DEPTH:2 * DEPTH], own.at[last:last + DEPTH], at(-1, 0)),
        halo(6, pack.at[0], from_behind.at[2, 0], at(-1, 1)),
        halo(7, pack.at[0], from_ahead.at[2, 0], at(-1, -1)),
    ]
    across = [
        halo(2, pack, from_behind.at[1], at(0, 1)),
        halo(3, pack, from_ahead.at[1], at(0, -1)),
    ]
    for copy in across:
        copy.start()

    @pl.when(has_up)
    def _():
        for copy in up:
            copy.start()

    @pl.when(has_down)
    def _():
        for copy in down:
            copy.start()

    low = (lane % 8) < 4

    def unpack(dr, group, rows, shift):
        joined = jnp.where(low, from_ahead[dr, group], from_behind[dr, group])
        for r in rows:
            for f in range(4):
                index = (r % 4) * 4 + f
                side[shift + r, f] = joined if index == 0 else pltpu.roll(joined, 128 - 8 * index, axis=1)

    for copy in across:
        copy.wait_recv()
    unpack(1, 0, range(0, 4), DEPTH)
    unpack(1, 1, range(4, 8), DEPTH)

    @pl.when(has_down)
    def _():
        for copy in up:
            copy.wait_recv()
        unpack(0, 1, range(radii - DEPTH, radii), DEPTH - radii)

    @pl.when(jnp.logical_not(has_down))
    def _():
        own[0:DEPTH] = jnp.zeros((DEPTH, 4, 8, 128), jnp.float32)
        side[0:DEPTH] = jnp.zeros((DEPTH, 4, 8, 128), jnp.float32)

    @pl.when(has_up)
    def _():
        for copy in down:
            copy.wait_recv()
        unpack(2, 0, range(0, DEPTH), last)

    @pl.when(jnp.logical_not(has_up))
    def _():
        own[last:last + DEPTH] = jnp.zeros((DEPTH, 4, 8, 128), jnp.float32)
        side[last:last + DEPTH] = jnp.zeros((DEPTH, 4, 8, 128), jnp.float32)

    def start_row(i):
        return jnp.concatenate([own[i, 0:3], side[i, 0:3]], axis=2)

    def row_facts(i):
        row = band * radii + i - DEPTH
        inside = jnp.logical_and(row >= 0, row < bands * radii)
        spin = rotation[jnp.clip(row, 0, bands * radii - 1)]
        return inside, spin, jnp.concatenate([own[i, 3], side[i, 3]], axis=1)

    def first_row(i, _):
        inside, spin, thick = row_facts(i)
        centre = start_row(i)
        rate = neighbour_rates(centre, start_row(i + 1), start_row(i - 1), thick, spin)
        first[i] = jnp.where(inside, centre + time_step * rate, 0.0)
        return 0

    lax.fori_loop(1, radii + 2 * DEPTH - 1, first_row, 0, unroll=True)

    def second_row(i, _):
        inside, spin, thick = row_facts(i)
        centre = first[i]
        rate = neighbour_rates(centre, first[i + 1], first[i - 1], thick, spin)
        second[i] = jnp.where(inside, 0.75 * start_row(i) + 0.25 * (centre + time_step * rate), 0.0)
        return 0

    lax.fori_loop(2, radii + 2 * DEPTH - 2, second_row, 0, unroll=True)

    def final_row(r, _):
        i = r + DEPTH
        inside, spin, thick = row_facts(i)
        centre = second[i]
        rate = neighbour_rates(centre, second[i + 1], second[i - 1], thick, spin)
        final[r] = own[i, 0:3] / 3.0 + 2.0 / 3.0 * (centre + time_step * rate)[..., :128]
        return 0

    per = radii // chunks

    def rows_of(c):
        return pl.ds(c * per, per)

    def pair_copy(c):
        mate = (band, sector + 1 - 2 * parity)
        return remote(final.at[rows_of(c)], partner.at[rows_of(c)], pair_sent.at[c], pair_got.at[c], mate)

    for c in range(chunks):
        lax.fori_loop(c * per, (c + 1) * per, final_row, 0, unroll=True)
        pair_copy(c).start()

    half = lax.broadcasted_iota(jnp.int32, (3, 8, 128), 2) < BLOCK

    def join_row(r):
        shift = shifts[0, band * radii + r]
        here, there = final[r], partner[r]
        left_own = (2 * parity - shift + 2 * sectors) % 4 // 2 == parity
        right_own = (2 * parity + 1 - shift + 2 * sectors) % 4 // 2 == parity
        odd = shift % 2 == 1
        here = jnp.where(odd, pltpu.roll(here, BLOCK, axis=2), here)
        there = jnp.where(odd, pltpu.roll(there, BLOCK, axis=2), there)
        take = jnp.where(half, left_own.astype(jnp.int32), right_own.astype(jnp.int32))
        lines[r // per][place, r % per] = jnp.where(take == 1, here, there)

    def line_copy(to_right, k, c):
        if to_right:
            held = lines[c].at[jnp.maximum(place - k, 0)]
            return remote(held, held, right_sent.at[k, c], right_got.at[k, c], at(0, 2))
        held = lines[c].at[jnp.minimum(place + k, places - 1)]
        return remote(held, held, left_sent.at[k, c], left_got.at[k, c], at(0, -2))

    def sends(to_right, k):
        if to_right:
            return jnp.logical_and(place < places - 1, place - k >= 0)
        return jnp.logical_and(place > 0, place + k < places)

    def gets(to_right, k):
        if to_right:
            return place - 1 - k >= 0
        return place + 1 + k < places

    def send(k, c):
        for to_right in (True, False):
            @pl.when(sends(to_right, k))
            def _():
                line_copy(to_right, k, c).start()

    def get(k, c):
        for to_right in (True, False):
            @pl.when(gets(to_right, k))
            def _():
                line_copy(to_right, k, c).wait_recv()

    for c in range(chunks):
        pair_copy(c).wait_recv()
        for r in range(c * per, (c + 1) * per):
            join_row(r)
        send(0, c)

    def forward(k, _):
        for c in range(chunks):
            get(k - 1, c)
            send(k, c)
        return 0

    if places <= 4:
        for k in range(1, places - 1):
            forward(k, 0)
    else:
        lax.fori_loop(1, places - 1, forward, 0)

    for c in range(chunks):
        if places > 1:
            get(places - 2, c)
        for r in range(c * per, (c + 1) * per):
            shift = shifts[0, band * radii + r]
            total = 2 * sectors
            left_from = (2 * sector - shift + total) % total // 4
            right_from = (2 * sector + 1 - shift + total) % total // 4
            moved = jnp.where(half, lines[c][left_from, r % per], lines[c][right_from, r % per])
            for f in range(3):
                out[f, pl.ds(r, 8, stride=8), :] = moved[f]

    for copy in across:
        copy.wait_send()

    @pl.when(has_up)
    def _():
        for copy in up:
            copy.wait_send()

    @pl.when(has_down)
    def _():
        for copy in down:
            copy.wait_send()

    for c in range(chunks):
        pair_copy(c).wait_send()

    def settle(k, _):
        for c in range(chunks):
            for to_right in (True, False):
                @pl.when(sends(to_right, k))
                def _():
                    line_copy(to_right, k, c).wait_send()
        return 0

    if places <= 4:
        for k in range(places - 1):
            settle(k, 0)
    else:
        lax.fori_loop(0, places - 1, settle, 0)


def body(fields, viscosity, rotation, shift_blocks):
    bands, sectors = lax.axis_size("rad"), lax.axis_size("azi")
    kinds, height, radii, width = fields.shape
    places, chunks = sectors // 2, 4
    rows = radii + 2 * DEPTH
    steps = max(places - 1, 1)
    vmem = lambda *shape: pltpu.VMEM(shape, jnp.float32)
    dma = lambda *shape: pltpu.SemaphoreType.DMA(shape)
    moved = pl.pallas_call(
        functools.partial(kernel, bands, sectors, chunks),
        out_shape=jax.ShapeDtypeStruct((kinds, height * radii, width), jnp.float32),
        in_specs=[
            pl.BlockSpec(memory_space=pltpu.VMEM),
            pl.BlockSpec(memory_space=pltpu.VMEM),
            pl.BlockSpec(memory_space=pltpu.SMEM),
            pl.BlockSpec(memory_space=pltpu.SMEM),
        ],
        out_specs=pl.BlockSpec(memory_space=pltpu.VMEM),
        scratch_shapes=[
            vmem(rows, 4, 8, 128), vmem(rows, 4, 8, 128),
            vmem(rows, 3, 8, 256), vmem(rows, 3, 8, 256),
            vmem(radii, 3, 8, 128), vmem(radii, 3, 8, 128),
            [vmem(places, radii // chunks, 3, 8, 128) for _ in range(chunks)],
            vmem(2, 8, 128), vmem(3, 2, 8, 128), vmem(3, 2, 8, 128),
            dma(8), dma(8), dma(chunks), dma(chunks),
            dma(steps, chunks), dma(steps, chunks), dma(steps, chunks), dma(steps, chunks),
        ],
        compiler_params=pltpu.CompilerParams(collective_id=0, has_side_effects=True, vmem_limit_bytes=24 * 2**20),
        name="disc_step",
    )(fields.reshape(kinds, height * radii, width), viscosity, rotation, shift_blocks)
    return moved.reshape(fields.shape)


def solution(mesh):
    return jax.shard_map(
        body,
        mesh=mesh,
        in_specs=(P(None, None, "rad", "azi"), P("rad", "azi"), P(), P()),
        out_specs=P(None, None, "rad", "azi"),
        check_vma=False,
    )
```

time: 71.4 us -> 28.3 us (0.40)
  the two profiles are of different devices: /device:TPU:2 before, /device:TPU:0 now
where the time goes in v1:
time: 28.3 us; the launch traced here: 28.1 us
  Pallas kernels  25.2 us (89%)
  local copies, waits for them, and re-layouts  2.89 us (10%)
    pallas_call x1, Pallas kernels, body(): pl.pallas_call(functools.partial(kernel, bands, sectors, chunks), out_sha...  25.2 us
    unnamed x9, local copies, waits for them, and re-layouts  2.89 us

profile of v1, /device:TPU:0, one launch (start us, length us, event | category | flops | bytes accessed | tf_op | source)
XLA Modules:
  0.0 28.1 jit_solution(11960398446229567195)
XLA Ops:
  0.0 0.0 copy-start.3
  0.0 0.0 copy-start.2
  0.0 0.7 %copy-done.3 = s32[1,32]{1,0:T(1,128)S(1)} copy-done((s32[1,32]{1,0:T(1,128)S(1)}, s32[1,32]{1,0:T(1,128)}, u32[]{:S(2)}) %copy-start.3) | copy-done | bytes 152
  0.7 0.0 copy-done.2
  0.7 0.0 copy-start
  0.7 0.9 %copy-done = f32[3,8,8,128]{3,2,1,0:T(8,128)S(1)} copy-done((f32[3,8,8,128]{3,2,1,0:T(8,128)S(1)}, f32[3,8,8,128]{3,2,1,0:T(8,128)}, u32[]{:S(2)}) %copy-start) | copy-done | bytes 98328
  1.6 0.0 copy-start.1
  1.6 0.7 %copy-done.1 = f32[8,128]{1,0:T(8,128)S(1)} copy-done((f32[8,128]{1,0:T(8,128)S(1)}, f32[8,128]{1,0:T(8,128)}, u32[]{:S(2)}) %copy-start.1) | copy-done | bytes 4120
  2.3 25.2 %disc_step.1 = f32[3,64,128]{2,1,0:T(8,128)S(1)} custom-call(f32[3,64,128]{2,1,0:T(8,128)S(1)} %bitcast.3, f32[8,128]{1,0:T(8,128)S(1)} %copy-done.1, f32[32]{0:T(128)S(1)} %copy-done.2, s32[1,32]{1,0:T(1,128)S(1)} %copy-done.3), custom_call_target="tpu_custom_call" | custom-call | tf_op jit(solution)/shard_map/disc_step/pallas_call | solution.py:304
  27.4 0.6 %copy.6 = f32[3,8,8,128]{3,2,1,0:T(8,128)} copy(f32[3,8,8,128]{3,2,1,0:T(8,128)S(1)} %bitcast.2) | data formatting | bytes 196608
Async XLA Ops:
  0.0 0.7 %copy-start.3 = (s32[1,32]{1,0:T(1,128)S(1)}, s32[1,32]{1,0:T(1,128)}, u32[]{:S(2)}) copy-start(s32[1,32]{1,0:T(1,128)} %shifts.1) | copy-start | bytes 388
  0.0 0.7 %copy-start.2 = (f32[32]{0:T(128)S(1)}, f32[32]{0:T(128)}, u32[]{:S(2)}) copy-start(f32[32]{0:T(128)} %rotation.1) | copy-start | bytes 388
  0.7 0.9 %copy-start = (f32[3,8,8,128]{3,2,1,0:T(8,128)S(1)}, f32[3,8,8,128]{3,2,1,0:T(8,128)}, u32[]{:S(2)}) copy-start(f32[3,8,8,128]{3,2,1,0:T(8,128)} %param.4) | copy-start | bytes 294916
  1.6 0.7 %copy-start.1 = (f32[8,128]{1,0:T(8,128)S(1)}, f32[8,128]{1,0:T(8,128)}, u32[]{:S(2)}) copy-start(f32[8,128]{1,0:T(8,128)} %viscosity.1) | copy-start | bytes 12292

commit v2 on v1

--- a/solution.py
+++ b/solution.py
@@ -31,8 +31,8 @@
 
 def kernel(
     bands, sectors, chunks,
-    fields, viscosity, rotation, shifts, out,
-    own, side, first, second, final, partner, lines, pack, from_ahead, from_behind,
+    fields_in, viscosity_in, rotation_in, shifts_in, out,
+    fields, viscosity, rotation, shifts, fetched, own, side, first, second, final, partner, lines, pack, from_ahead, from_behind,
     halo_sent, halo_got, pair_sent, pair_got, right_sent, right_got, left_sent, left_got,
 ):
     radii = viscosity.shape[0]
@@ -49,6 +49,17 @@
     greeted = [(dr, da) for dr in (-1, 0, 1) for da in (-1, 0, 1) if (dr, da) != (0, 0)] + [(0, -2), (0, 2)]
     for dr, da in greeted:
         pl.semaphore_signal(barrier, inc=1, device_id=at(dr, da), device_id_type=MESH)
+
+    fetches = [
+        pltpu.make_async_copy(src, dst, fetched.at[i])
+        for i, (src, dst) in enumerate(
+            [(fields_in, fields), (viscosity_in, viscosity), (rotation_in, rotation), (shifts_in, shifts)]
+        )
+    ]
+    for fetch in fetches:
+        fetch.start()
+    for fetch in fetches:
+        fetch.wait()
 
     lane = lax.broadcasted_iota(jnp.int32, (8, 128), 1)
     slot = ((lane + 4) // 8) % 16
@@ -304,14 +315,11 @@
     moved = pl.pallas_call(
         functools.partial(kernel, bands, sectors, chunks),
         out_shape=jax.ShapeDtypeStruct((kinds, height * radii, width), jnp.float32),
-        in_specs=[
-            pl.BlockSpec(memory_space=pltpu.VMEM),
-            pl.BlockSpec(memory_space=pltpu.VMEM),
-            pl.BlockSpec(memory_space=pltpu.SMEM),
-            pl.BlockSpec(memory_space=pltpu.SMEM),
-        ],
+        in_specs=[pl.BlockSpec(memory_space=pltpu.HBM)] * 4,
         out_specs=pl.BlockSpec(memory_space=pltpu.VMEM),
         scratch_shapes=[
+            vmem(kinds, height * radii, width), vmem(radii, width),
+            pltpu.SMEM(rotation.shape, jnp.float32), pltpu.SMEM(shift_blocks.shape, jnp.int32), dma(4),
             vmem(rows, 4, 8, 128), vmem(rows, 4, 8, 128),
             vmem(rows, 3, 8, 256), vmem(rows, 3, 8, 256),
             vmem(radii, 3, 8, 128), vmem(radii, 3, 8, 128),
@@ -320,7 +328,7 @@
             dma(8), dma(8), dma(chunks), dma(chunks),
             dma(steps, chunks), dma(steps, chunks), dma(steps, chunks), dma(steps, chunks),
         ],
-        compiler_params=pltpu.CompilerParams(collective_id=0, has_side_effects=True, vmem_limit_bytes=24 * 2**20),
+        compiler_params=pltpu.CompilerParams(collective_id=0, has_side_effects=True, vmem_limit_bytes=56 * 2**20),
         name="disc_step",
     )(fields.reshape(kinds, height * radii, width), viscosity, rotation, shift_blocks)
     return moved.reshape(fields.shape)

time: 28.3 us -> 26.9 us (0.951)
  local copies, waits for them, and re-layouts: 2.89 us -> 1.54 us
    unnamed x9 -> x1, local copies, waits for them, and re-layouts: 2.89 us -> 1.54 us
where the time goes in v2:
time: 26.9 us; the launch traced here: 26.8 us
  Pallas kernels  25.2 us (94%)
  local copies, waits for them, and re-layouts  1.54 us (6%)
    pallas_call x1, Pallas kernels, body(): pl.pallas_call(functools.partial(kernel, bands, sectors, chunks), out_sha...  25.2 us
    unnamed x1, local copies, waits for them, and re-layouts  1.54 us

profile of v2, /device:TPU:0, one launch (start us, length us, event | category | flops | bytes accessed | tf_op | source)
XLA Modules:
  0.0 26.8 jit_solution(11961815207672173921)
XLA Ops:
  0.0 25.2 %disc_step.1 = f32[3,64,128]{2,1,0:T(8,128)} custom-call(f32[3,64,128]{2,1,0:T(8,128)} %bitcast.3, f32[8,128]{1,0:T(8,128)} %viscosity_in.1, f32[32]{0:T(128)} %rotation_in.1, s32[1,32]{1,0:T(1,128)} %shifts_in.1), custom_call_target="tpu_custom_call" | custom-call | tf_op jit(solution)/shard_map/disc_step/pallas_call | solution.py:315
  25.2 1.5 %copy.6 = f32[3,8,8,128]{3,2,1,0:T(8,128)} copy(f32[3,8,8,128]{3,2,1,0:T(8,128)} %bitcast.2) | data formatting | bytes 196608

commit v3 on v2

--- a/solution.py
+++ b/solution.py
@@ -32,7 +32,7 @@
 def kernel(
     bands, sectors, chunks,
     fields_in, viscosity_in, rotation_in, shifts_in, out,
-    fields, viscosity, rotation, shifts, fetched, own, side, first, second, final, partner, lines, pack, from_ahead, from_behind,
+    fields, viscosity, rotation, shifts, fetched, own, side, first, second, final, partner, lefts, rights, merged, pack, from_ahead, from_behind,
     halo_sent, halo_got, pair_sent, pair_got, right_sent, right_got, left_sent, left_got,
 ):
     radii = viscosity.shape[0]
@@ -212,24 +212,37 @@
         here = jnp.where(odd, pltpu.roll(here, BLOCK, axis=2), here)
         there = jnp.where(odd, pltpu.roll(there, BLOCK, axis=2), there)
         take = jnp.where(half, left_own.astype(jnp.int32), right_own.astype(jnp.int32))
-        lines[r // per][place, r % per] = jnp.where(take == 1, here, there)
+        joined = jnp.where(take == 1, here, there)
+        lefts[r // per][place, r % per] = joined
+        rights[r // per][place, r % per] = joined
 
     def line_copy(to_right, k, c):
         if to_right:
-            held = lines[c].at[jnp.maximum(place - k, 0)]
+            held = lefts[c].at[jnp.maximum(place - k, 0)]
             return remote(held, held, right_sent.at[k, c], right_got.at[k, c], at(0, 2))
-        held = lines[c].at[jnp.minimum(place + k, places - 1)]
+        held = rights[c].at[jnp.minimum(place + k, places - 1)]
         return remote(held, held, left_sent.at[k, c], left_got.at[k, c], at(0, -2))
+
+    def end_copy(to_right, c):
+        if to_right:
+            return remote(merged.at[0, c], lefts[c].at[place], right_sent.at[0, c], right_got.at[0, c], at(0, 2))
+        return remote(merged.at[1, c], rights[c].at[place], left_sent.at[0, c], left_got.at[0, c], at(0, -2))
+
+    def ends(to_right):
+        return place == places - 2 if to_right else place == 1
 
     def sends(to_right, k):
         if to_right:
-            return jnp.logical_and(place < places - 1, place - k >= 0)
-        return jnp.logical_and(place > 0, place + k < places)
+            return jnp.logical_and(place < places - 2, place - k >= 0)
+        return jnp.logical_and(place > 1, place + k < places)
 
     def gets(to_right, k):
         if to_right:
-            return place - 1 - k >= 0
-        return place + 1 + k < places
+            return jnp.logical_and(place < places - 1, place - 1 - k >= 0)
+        return jnp.logical_and(place > 0, place + 1 + k < places)
+
+    def gets_end(to_right):
+        return place == places - 1 if to_right else place == 0
 
     def send(k, c):
         for to_right in (True, False):
@@ -242,6 +255,25 @@
             @pl.when(gets(to_right, k))
             def _():
                 line_copy(to_right, k, c).wait_recv()
+
+    def sources(r, target):
+        shift = shifts[0, band * radii + r]
+        total = 2 * sectors
+        return [(2 * target + h - shift + total) % total // 4 for h in range(2)]
+
+    def send_end(c):
+        for to_right in (True, False):
+            @pl.when(ends(to_right))
+            def _():
+                for r in range(c * per, (c + 1) * per):
+                    target = sector + 2 if to_right else sector - 2
+                    first_from, second_from = sources(r, target)
+                    if to_right:
+                        pick = lambda at_place: lefts[c][jnp.minimum(at_place, place), r % per]
+                    else:
+                        pick = lambda at_place: rights[c][jnp.maximum(at_place, place), r % per]
+                    merged[1 - int(to_right), c, r % per] = jnp.where(half, pick(first_from), pick(second_from))
+                end_copy(to_right, c).start()
 
     for c in range(chunks):
         pair_copy(c).wait_recv()
@@ -256,20 +288,30 @@
         return 0
 
     if places <= 4:
-        for k in range(1, places - 1):
+        for k in range(1, places - 2):
             forward(k, 0)
     else:
-        lax.fori_loop(1, places - 1, forward, 0)
-
-    for c in range(chunks):
-        if places > 1:
-            get(places - 2, c)
+        lax.fori_loop(1, places - 2, forward, 0)
+
+    for c in range(chunks):
+        get(places - 3, c)
+        send_end(c)
+
+    for c in range(chunks):
+        for to_right in (True, False):
+            @pl.when(gets_end(to_right))
+            def _():
+                end_copy(to_right, c).wait_recv()
         for r in range(c * per, (c + 1) * per):
-            shift = shifts[0, band * radii + r]
-            total = 2 * sectors
-            left_from = (2 * sector - shift + total) % total // 4
-            right_from = (2 * sector + 1 - shift + total) % total // 4
-            moved = jnp.where(half, lines[c][left_from, r % per], lines[c][right_from, r % per])
+            def pick(at_place):
+                near = jnp.where(place == places - 1, places - 2, at_place)
+                left = jnp.where(at_place >= place, place, near)
+                far = jnp.where(place == 0, 1, at_place)
+                right = jnp.where(at_place <= place, place, far)
+                return jnp.where(at_place <= place, lefts[c][left, r % per], rights[c][right, r % per])
+
+            first_from, second_from = sources(r, sector)
+            moved = jnp.where(half, pick(first_from), pick(second_from))
             for f in range(3):
                 out[f, pl.ds(r, 8, stride=8), :] = moved[f]
 
@@ -288,6 +330,12 @@
 
     for c in range(chunks):
         pair_copy(c).wait_send()
+
+    for c in range(chunks):
+        for to_right in (True, False):
+            @pl.when(ends(to_right))
+            def _():
+                end_copy(to_right, c).wait_send()
 
     def settle(k, _):
         for c in range(chunks):
@@ -298,10 +346,10 @@
         return 0
 
     if places <= 4:
-        for k in range(places - 1):
+        for k in range(places - 2):
             settle(k, 0)
     else:
-        lax.fori_loop(0, places - 1, settle, 0)
+        lax.fori_loop(0, places - 2, settle, 0)
 
 
 def body(fields, viscosity, rotation, shift_blocks):
@@ -309,12 +357,12 @@
     kinds, height, radii, width = fields.shape
     places, chunks = sectors // 2, 4
     rows = radii + 2 * DEPTH
-    steps = max(places - 1, 1)
+    steps = places - 2
     vmem = lambda *shape: pltpu.VMEM(shape, jnp.float32)
     dma = lambda *shape: pltpu.SemaphoreType.DMA(shape)
     moved = pl.pallas_call(
         functools.partial(kernel, bands, sectors, chunks),
-        out_shape=jax.ShapeDtypeStruct((kinds, height * radii, width), jnp.float32),
+        out_shape=pltpu.VMEM((kinds, height * radii, width), jnp.float32),
         in_specs=[pl.BlockSpec(memory_space=pltpu.HBM)] * 4,
         out_specs=pl.BlockSpec(memory_space=pltpu.VMEM),
         scratch_shapes=[
@@ -324,6 +372,8 @@
             vmem(rows, 3, 8, 256), vmem(rows, 3, 8, 256),
             vmem(radii, 3, 8, 128), vmem(radii, 3, 8, 128),
             [vmem(places, radii // chunks, 3, 8, 128) for _ in range(chunks)],
+            [vmem(places, radii // chunks, 3, 8, 128) for _ in range(chunks)],
+            vmem(2, chunks, radii // chunks, 3, 8, 128),
             vmem(2, 8, 128), vmem(3, 2, 8, 128), vmem(3, 2, 8, 128),
             dma(8), dma(8), dma(chunks), dma(chunks),
             dma(steps, chunks), dma(steps, chunks), dma(steps, chunks), dma(steps, chunks),

time: 26.9 us -> 25.3 us (0.941)
  local copies, waits for them, and re-layouts: 1.54 us -> 0.64 us
  Pallas kernels: 25.2 us -> 24.5 us
    unnamed x1, local copies, waits for them, and re-layouts: 1.54 us -> 0.64 us
    pallas_call x1, Pallas kernels: 25.2 us -> 24.5 us  [body(): pl.pallas_call(functools.partial(kernel, bands, sectors, chunks), out_sha...]
where the time goes in v3:
time: 25.3 us; the launch traced here: 25.1 us
  Pallas kernels  24.5 us (97%)
  local copies, waits for them, and re-layouts  0.64 us (3%)
    pallas_call x1, Pallas kernels, body(): pl.pallas_call(functools.partial(kernel, bands, sectors, chunks), out_sha...  24.5 us
    unnamed x1, local copies, waits for them, and re-layouts  0.64 us

profile of v3, /device:TPU:0, one launch (start us, length us, event | category | flops | bytes accessed | tf_op | source)
XLA Modules:
  0.0 25.1 jit_solution(17368164859913534608)
XLA Ops:
  0.0 24.5 %disc_step.1 = f32[3,64,128]{2,1,0:T(8,128)S(1)} custom-call(f32[3,64,128]{2,1,0:T(8,128)} %bitcast.3, f32[8,128]{1,0:T(8,128)} %viscosity_in.1, f32[32]{0:T(128)} %rotation_in.1, s32[1,32]{1,0:T(1,128)} %shifts_in.1), custom_call_target="tpu_custom_call" | custom-call | tf_op jit(solution)/shard_map/disc_step/pallas_call | solution.py:363
  24.5 0.6 %copy.6 = f32[3,8,8,128]{3,2,1,0:T(8,128)} copy(f32[3,8,8,128]{3,2,1,0:T(8,128)S(1)} %bitcast.2) | data formatting | bytes 196608

commit v4 on v3

--- a/solution.py
+++ b/solution.py
@@ -46,7 +46,8 @@
         return (lax.rem(band + dr + bands, bands), lax.rem(sector + da + sectors, sectors))
 
     barrier = pltpu.get_barrier_semaphore()
-    greeted = [(dr, da) for dr in (-1, 0, 1) for da in (-1, 0, 1) if (dr, da) != (0, 0)] + [(0, -2), (0, 2)]
+    greeted = [(dr, da) for dr in (-1, 0, 1) for da in (-1, 0, 1) if (dr, da) != (0, 0)]
+    greeted += [(0, 2 * d - sectors) for d in range(1, places)]
     for dr, da in greeted:
         pl.semaphore_signal(barrier, inc=1, device_id=at(dr, da), device_id_type=MESH)
 
@@ -216,12 +217,12 @@
         lefts[r // per][place, r % per] = joined
         rights[r // per][place, r % per] = joined
 
-    def line_copy(to_right, k, c):
+    def line_copy(to_right, d, c):
         if to_right:
-            held = lefts[c].at[jnp.maximum(place - k, 0)]
-            return remote(held, held, right_sent.at[k, c], right_got.at[k, c], at(0, 2))
-        held = rights[c].at[jnp.minimum(place + k, places - 1)]
-        return remote(held, held, left_sent.at[k, c], left_got.at[k, c], at(0, -2))
+            held = lefts[c].at[place]
+            return remote(held, held, right_sent.at[d, c], right_got.at[d, c], at(0, 2 * d))
+        held = rights[c].at[place]
+        return remote(held, held, left_sent.at[d, c], left_got.at[d, c], at(0, -2 * d))
 
     def end_copy(to_right, c):
         if to_right:
@@ -231,30 +232,29 @@
     def ends(to_right):
         return place == places - 2 if to_right else place == 1
 
-    def sends(to_right, k):
-        if to_right:
-            return jnp.logical_and(place < places - 2, place - k >= 0)
-        return jnp.logical_and(place > 1, place + k < places)
-
-    def gets(to_right, k):
-        if to_right:
-            return jnp.logical_and(place < places - 1, place - 1 - k >= 0)
-        return jnp.logical_and(place > 0, place + 1 + k < places)
+    def sends(to_right, d):
+        return place + d <= places - 2 if to_right else place - d >= 1
+
+    def gets(to_right, d):
+        inner = jnp.logical_and(place >= 1, place <= places - 2)
+        return jnp.logical_and(inner, place - d >= 0 if to_right else place + d <= places - 1)
 
     def gets_end(to_right):
         return place == places - 1 if to_right else place == 0
 
-    def send(k, c):
-        for to_right in (True, False):
-            @pl.when(sends(to_right, k))
-            def _():
-                line_copy(to_right, k, c).start()
-
-    def get(k, c):
-        for to_right in (True, False):
-            @pl.when(gets(to_right, k))
-            def _():
-                line_copy(to_right, k, c).wait_recv()
+    def send(c):
+        for d in range(places - 2, 0, -1):
+            for to_right in (True, False):
+                @pl.when(sends(to_right, d))
+                def _():
+                    line_copy(to_right, d, c).start()
+
+    def get(c):
+        for d in range(1, places - 1):
+            for to_right in (True, False):
+                @pl.when(gets(to_right, d))
+                def _():
+                    line_copy(to_right, d, c).wait_recv()
 
     def sources(r, target):
         shift = shifts[0, band * radii + r]
@@ -279,22 +279,10 @@
         pair_copy(c).wait_recv()
         for r in range(c * per, (c + 1) * per):
             join_row(r)
-        send(0, c)
-
-    def forward(k, _):
-        for c in range(chunks):
-            get(k - 1, c)
-            send(k, c)
-        return 0
-
-    if places <= 4:
-        for k in range(1, places - 2):
-            forward(k, 0)
-    else:
-        lax.fori_loop(1, places - 2, forward, 0)
-
-    for c in range(chunks):
-        get(places - 3, c)
+        send(c)
+
+    for c in range(chunks):
+        get(c)
         send_end(c)
 
     for c in range(chunks):
@@ -337,19 +325,12 @@
             def _():
                 end_copy(to_right, c).wait_send()
 
-    def settle(k, _):
+    for d in range(1, places - 1):
         for c in range(chunks):
             for to_right in (True, False):
-                @pl.when(sends(to_right, k))
+                @pl.when(sends(to_right, d))
                 def _():
-                    line_copy(to_right, k, c).wait_send()
-        return 0
-
-    if places <= 4:
-        for k in range(places - 2):
-            settle(k, 0)
-    else:
-        lax.fori_loop(0, places - 2, settle, 0)
+                    line_copy(to_right, d, c).wait_send()
 
 
 def body(fields, viscosity, rotation, shift_blocks):
@@ -357,7 +338,7 @@
     kinds, height, radii, width = fields.shape
     places, chunks = sectors // 2, 4
     rows = radii + 2 * DEPTH
-    steps = places - 2
+    steps = places - 1
     vmem = lambda *shape: pltpu.VMEM(shape, jnp.float32)
     dma = lambda *shape: pltpu.SemaphoreType.DMA(shape)
     moved = pl.pallas_call(

time: 25.3 us -> 24.2 us (0.957)
  Pallas kernels: 24.5 us -> 23.4 us
    pallas_call x1, Pallas kernels: 24.5 us -> 23.4 us  [body(): pl.pallas_call(functools.partial(kernel, bands, sectors, chunks), out_sha...]
where the time goes in v4:
time: 24.2 us; the launch traced here: 24.1 us
  Pallas kernels  23.4 us (97%)
  local copies, waits for them, and re-layouts  0.64 us (3%)
    pallas_call x1, Pallas kernels, body(): pl.pallas_call(functools.partial(kernel, bands, sectors, chunks), out_sha...  23.4 us
    unnamed x1, local copies, waits for them, and re-layouts  0.64 us

profile of v4, /device:TPU:0, one launch (start us, length us, event | category | flops | bytes accessed | tf_op | source)
XLA Modules:
  0.0 24.1 jit_solution(10040609550796576201)
XLA Ops:
  0.0 23.4 %disc_step.1 = f32[3,64,128]{2,1,0:T(8,128)S(1)} custom-call(f32[3,64,128]{2,1,0:T(8,128)} %bitcast.3, f32[8,128]{1,0:T(8,128)} %viscosity_in.1, f32[32]{0:T(128)} %rotation_in.1, s32[1,32]{1,0:T(1,128)} %shifts_in.1), custom_call_target="tpu_custom_call" | custom-call | tf_op jit(solution)/shard_map/disc_step/pallas_call | solution.py:344
  23.4 0.6 %copy.6 = f32[3,8,8,128]{3,2,1,0:T(8,128)} copy(f32[3,8,8,128]{3,2,1,0:T(8,128)S(1)} %bitcast.2) | data formatting | bytes 196608

commit v5 on v4

--- a/solution.py
+++ b/solution.py
@@ -242,10 +242,13 @@
     def gets_end(to_right):
         return place == places - 1 if to_right else place == 0
 
-    def send(c):
+    def send(c, urgent):
         for d in range(places - 2, 0, -1):
             for to_right in (True, False):
-                @pl.when(sends(to_right, d))
+                far = place + d == places - 2 if to_right else place - d == 1
+                wanted = far if urgent else jnp.logical_not(far)
+
+                @pl.when(jnp.logical_and(sends(to_right, d), wanted))
                 def _():
                     line_copy(to_right, d, c).start()
 
@@ -279,7 +282,10 @@
         pair_copy(c).wait_recv()
         for r in range(c * per, (c + 1) * per):
             join_row(r)
-        send(c)
+        send(c, True)
+
+    for c in range(chunks):
+        send(c, False)
 
     for c in range(chunks):
         get(c)

time: 24.2 us -> 23.7 us (0.979)
  Pallas kernels: 23.4 us -> 22.9 us
    pallas_call x1, Pallas kernels: 23.4 us -> 22.9 us  [body(): pl.pallas_call(functools.partial(kernel, bands, sectors, chunks), out_sha...]
where the time goes in v5:
time: 23.7 us; the launch traced here: 23.6 us
  Pallas kernels  22.9 us (97%)
  local copies, waits for them, and re-layouts  0.64 us (3%)
    pallas_call x1, Pallas kernels, body(): pl.pallas_call(functools.partial(kernel, bands, sectors, chunks), out_sha...  22.9 us
    unnamed x1, local copies, waits for them, and re-layouts  0.64 us

profile of v5, /device:TPU:0, one launch (start us, length us, event | category | flops | bytes accessed | tf_op | source)
XLA Modules:
  0.0 23.6 jit_solution(16876639291172002631)
XLA Ops:
  0.0 22.9 %disc_step.1 = f32[3,64,128]{2,1,0:T(8,128)S(1)} custom-call(f32[3,64,128]{2,1,0:T(8,128)} %bitcast.3, f32[8,128]{1,0:T(8,128)} %viscosity_in.1, f32[32]{0:T(128)} %rotation_in.1, s32[1,32]{1,0:T(1,128)} %shifts_in.1), custom_call_target="tpu_custom_call" | custom-call | tf_op jit(solution)/shard_map/disc_step/pallas_call | solution.py:350
  22.9 0.6 %copy.6 = f32[3,8,8,128]{3,2,1,0:T(8,128)} copy(f32[3,8,8,128]{3,2,1,0:T(8,128)S(1)} %bitcast.2) | data formatting | bytes 196608

commit v6 on v5

--- a/solution.py
+++ b/solution.py
@@ -252,10 +252,12 @@
                 def _():
                     line_copy(to_right, d, c).start()
 
-    def get(c):
+    def get(c, urgent):
         for d in range(1, places - 1):
             for to_right in (True, False):
-                @pl.when(gets(to_right, d))
+                wanted = ends(to_right) if urgent else jnp.logical_not(ends(to_right))
+
+                @pl.when(jnp.logical_and(gets(to_right, d), wanted))
                 def _():
                     line_copy(to_right, d, c).wait_recv()
 
@@ -288,10 +290,11 @@
         send(c, False)
 
     for c in range(chunks):
-        get(c)
+        get(c, True)
         send_end(c)
 
     for c in range(chunks):
+        get(c, False)
         for to_right in (True, False):
             @pl.when(gets_end(to_right))
             def _():

time: 23.7 us -> 23.7 us (level)
  no operation moved by 1% of the time
where the time goes in v6:
time: 23.7 us; the launch traced here: 23.5 us
  Pallas kernels  22.9 us (97%)
  local copies, waits for them, and re-layouts  0.64 us (3%)
    pallas_call x1, Pallas kernels, body(): pl.pallas_call(functools.partial(kernel, bands, sectors, chunks), out_sha...  22.9 us
    unnamed x1, local copies, waits for them, and re-layouts  0.64 us

profile of v6, /device:TPU:0, one launch (start us, length us, event | category | flops | bytes accessed | tf_op | source)
XLA Modules:
  0.0 23.5 jit_solution(5747037200922466633)
XLA Ops:
  0.0 22.9 %disc_step.1 = f32[3,64,128]{2,1,0:T(8,128)S(1)} custom-call(f32[3,64,128]{2,1,0:T(8,128)} %bitcast.3, f32[8,128]{1,0:T(8,128)} %viscosity_in.1, f32[32]{0:T(128)} %rotation_in.1, s32[1,32]{1,0:T(1,128)} %shifts_in.1), custom_call_target="tpu_custom_call" | custom-call | tf_op jit(solution)/shard_map/disc_step/pallas_call | solution.py:353
  22.9 0.6 %copy.6 = f32[3,8,8,128]{3,2,1,0:T(8,128)} copy(f32[3,8,8,128]{3,2,1,0:T(8,128)S(1)} %bitcast.2) | data formatting | bytes 196608

commit v7 on v4

--- a/solution.py
+++ b/solution.py
@@ -32,8 +32,8 @@
 def kernel(
     bands, sectors, chunks,
     fields_in, viscosity_in, rotation_in, shifts_in, out,
-    fields, viscosity, rotation, shifts, fetched, own, side, first, second, final, partner, lefts, rights, merged, pack, from_ahead, from_behind,
-    halo_sent, halo_got, pair_sent, pair_got, right_sent, right_got, left_sent, left_got,
+    fields, viscosity, rotation, shifts, fetched, own, side, first, second, raws, gots, staged, pack, from_ahead, from_behind,
+    halo_sent, halo_got, mate_sent, mate_got, end_sent, end_got, right_sent, right_got, left_sent, left_got,
 ):
     radii = viscosity.shape[0]
     places = sectors // 2
@@ -47,7 +47,7 @@
 
     barrier = pltpu.get_barrier_semaphore()
     greeted = [(dr, da) for dr in (-1, 0, 1) for da in (-1, 0, 1) if (dr, da) != (0, 0)]
-    greeted += [(0, 2 * d - sectors) for d in range(1, places)]
+    greeted += [(0, 2 * d - sectors) for d in range(1, places)] + [(0, -3), (0, 3)]
     for dr, da in greeted:
         pl.semaphore_signal(barrier, inc=1, device_id=at(dr, da), device_id_type=MESH)
 
@@ -181,56 +181,20 @@
 
     lax.fori_loop(2, radii + 2 * DEPTH - 2, second_row, 0, unroll=True)
 
-    def final_row(r, _):
+    per = radii // chunks
+
+    def final_row(c, r):
         i = r + DEPTH
         inside, spin, thick = row_facts(i)
         centre = second[i]
         rate = neighbour_rates(centre, second[i + 1], second[i - 1], thick, spin)
-        final[r] = own[i, 0:3] / 3.0 + 2.0 / 3.0 * (centre + time_step * rate)[..., :128]
-        return 0
-
-    per = radii // chunks
-
-    def rows_of(c):
-        return pl.ds(c * per, per)
-
-    def pair_copy(c):
-        mate = (band, sector + 1 - 2 * parity)
-        return remote(final.at[rows_of(c)], partner.at[rows_of(c)], pair_sent.at[c], pair_got.at[c], mate)
-
-    for c in range(chunks):
-        lax.fori_loop(c * per, (c + 1) * per, final_row, 0, unroll=True)
-        pair_copy(c).start()
-
-    half = lax.broadcasted_iota(jnp.int32, (3, 8, 128), 2) < BLOCK
-
-    def join_row(r):
-        shift = shifts[0, band * radii + r]
-        here, there = final[r], partner[r]
-        left_own = (2 * parity - shift + 2 * sectors) % 4 // 2 == parity
-        right_own = (2 * parity + 1 - shift + 2 * sectors) % 4 // 2 == parity
-        odd = shift % 2 == 1
-        here = jnp.where(odd, pltpu.roll(here, BLOCK, axis=2), here)
-        there = jnp.where(odd, pltpu.roll(there, BLOCK, axis=2), there)
-        take = jnp.where(half, left_own.astype(jnp.int32), right_own.astype(jnp.int32))
-        joined = jnp.where(take == 1, here, there)
-        lefts[r // per][place, r % per] = joined
-        rights[r // per][place, r % per] = joined
+        raws[c][place, r - c * per] = own[i, 0:3] / 3.0 + 2.0 / 3.0 * (centre + time_step * rate)[..., :128]
 
     def line_copy(to_right, d, c):
+        held = raws[c].at[place]
         if to_right:
-            held = lefts[c].at[place]
             return remote(held, held, right_sent.at[d, c], right_got.at[d, c], at(0, 2 * d))
-        held = rights[c].at[place]
         return remote(held, held, left_sent.at[d, c], left_got.at[d, c], at(0, -2 * d))
-
-    def end_copy(to_right, c):
-        if to_right:
-            return remote(merged.at[0, c], lefts[c].at[place], right_sent.at[0, c], right_got.at[0, c], at(0, 2))
-        return remote(merged.at[1, c], rights[c].at[place], left_sent.at[0, c], left_got.at[0, c], at(0, -2))
-
-    def ends(to_right):
-        return place == places - 2 if to_right else place == 1
 
     def sends(to_right, d):
         return place + d <= places - 2 if to_right else place - d >= 1
@@ -238,9 +202,6 @@
     def gets(to_right, d):
         inner = jnp.logical_and(place >= 1, place <= places - 2)
         return jnp.logical_and(inner, place - d >= 0 if to_right else place + d <= places - 1)
-
-    def gets_end(to_right):
-        return place == places - 1 if to_right else place == 0
 
     def send(c):
         for d in range(places - 2, 0, -1):
@@ -256,50 +217,77 @@
                 def _():
                     line_copy(to_right, d, c).wait_recv()
 
+    for c in range(chunks):
+        for r in range(c * per, (c + 1) * per):
+            final_row(c, r)
+        send(c)
+
+    half = lax.broadcasted_iota(jnp.int32, (3, 8, 128), 2) < BLOCK
+    total = 2 * sectors
+
     def sources(r, target):
         shift = shifts[0, band * radii + r]
-        total = 2 * sectors
-        return [(2 * target + h - shift + total) % total // 4 for h in range(2)]
-
-    def send_end(c):
-        for to_right in (True, False):
-            @pl.when(ends(to_right))
-            def _():
-                for r in range(c * per, (c + 1) * per):
-                    target = sector + 2 if to_right else sector - 2
-                    first_from, second_from = sources(r, target)
-                    if to_right:
-                        pick = lambda at_place: lefts[c][jnp.minimum(at_place, place), r % per]
-                    else:
-                        pick = lambda at_place: rights[c][jnp.maximum(at_place, place), r % per]
-                    merged[1 - int(to_right), c, r % per] = jnp.where(half, pick(first_from), pick(second_from))
-                end_copy(to_right, c).start()
-
-    for c in range(chunks):
-        pair_copy(c).wait_recv()
-        for r in range(c * per, (c + 1) * per):
-            join_row(r)
-        send(c)
+        to_first = (2 * target - shift + total) % total // 2
+        to_second = (2 * target + 1 - shift + total) % total // 2
+        odd = shift % 2 == 1
+        return jnp.where(odd, to_second, to_first), jnp.where(odd, to_first, to_second), odd
+
+    def picked(c, r, target):
+        low_from, high_from, _ = sources(r, target)
+        return jnp.where(half, raws[c][low_from // 2, r - c * per], raws[c][high_from // 2, r - c * per])
+
+    inner = jnp.logical_and(place >= 1, place <= places - 2)
+    outer = jnp.logical_not(inner)
+    beside = jnp.logical_or(place == 1, place == places - 2)
+    mate = sector + 1 - 2 * parity
+    end = sector + jnp.where(place == 1, -2, 2)
+    end_mate = end + 1 - 2 * parity
+
+    def mate_copy(c):
+        return remote(staged.at[0, c], gots[c].at[parity], mate_sent.at[c], mate_got.at[c], (band, mate))
+
+    def end_copy(other, c):
+        target = lax.rem((end_mate if other else end) + sectors, sectors)
+        return remote(
+            staged.at[1 + other, c], gots[c].at[parity], end_sent.at[other, c], end_got.at[parity, c], (band, target)
+        )
+
+    def from_helper(q, c):
+        return remote(gots[c].at[q], gots[c].at[q], end_sent.at[q, c], end_got.at[q, c], (band, mate))
 
     for c in range(chunks):
         get(c)
-        send_end(c)
+        rows = range(c * per, (c + 1) * per)
+
+        @pl.when(beside)
+        def _():
+            for other, target in ((0, end), (1, end_mate)):
+                for r in rows:
+                    staged[1 + other, c, r - c * per] = picked(c, r, target)
+                end_copy(other, c).start()
+
+        @pl.when(inner)
+        def _():
+            for r in rows:
+                staged[0, c, r - c * per] = picked(c, r, mate)
+            mate_copy(c).start()
+            for r in rows:
+                gots[c][parity, r - c * per] = picked(c, r, sector)
 
     for c in range(chunks):
-        for to_right in (True, False):
-            @pl.when(gets_end(to_right))
-            def _():
-                end_copy(to_right, c).wait_recv()
+        @pl.when(inner)
+        def _():
+            mate_copy(c).wait_recv()
+
+        @pl.when(outer)
+        def _():
+            for q in range(2):
+                from_helper(q, c).wait_recv()
+
         for r in range(c * per, (c + 1) * per):
-            def pick(at_place):
-                near = jnp.where(place == places - 1, places - 2, at_place)
-                left = jnp.where(at_place >= place, place, near)
-                far = jnp.where(place == 0, 1, at_place)
-                right = jnp.where(at_place <= place, place, far)
-                return jnp.where(at_place <= place, lefts[c][left, r % per], rights[c][right, r % per])
-
-            first_from, second_from = sources(r, sector)
-            moved = jnp.where(half, pick(first_from), pick(second_from))
+            low_from, high_from, odd = sources(r, sector)
+            moved = jnp.where(half, gots[c][low_from % 2, r - c * per], gots[c][high_from % 2, r - c * per])
+            moved = jnp.where(odd, pltpu.roll(moved, BLOCK, axis=2), moved)
             for f in range(3):
                 out[f, pl.ds(r, 8, stride=8), :] = moved[f]
 
@@ -317,13 +305,14 @@
             copy.wait_send()
 
     for c in range(chunks):
-        pair_copy(c).wait_send()
-
-    for c in range(chunks):
-        for to_right in (True, False):
-            @pl.when(ends(to_right))
-            def _():
-                end_copy(to_right, c).wait_send()
+        @pl.when(beside)
+        def _():
+            for other in range(2):
+                end_copy(other, c).wait_send()
+
+        @pl.when(inner)
+        def _():
+            mate_copy(c).wait_send()
 
     for d in range(1, places - 1):
         for c in range(chunks):
@@ -351,12 +340,11 @@
             pltpu.SMEM(rotation.shape, jnp.float32), pltpu.SMEM(shift_blocks.shape, jnp.int32), dma(4),
             vmem(rows, 4, 8, 128), vmem(rows, 4, 8, 128),
             vmem(rows, 3, 8, 256), vmem(rows, 3, 8, 256),
-            vmem(radii, 3, 8, 128), vmem(radii, 3, 8, 128),
             [vmem(places, radii // chunks, 3, 8, 128) for _ in range(chunks)],
-            [vmem(places, radii // chunks, 3, 8, 128) for _ in range(chunks)],
-            vmem(2, chunks, radii // chunks, 3, 8, 128),
+            [vmem(2, radii // chunks, 3, 8, 128) for _ in range(chunks)],
+            vmem(3, chunks, radii // chunks, 3, 8, 128),
             vmem(2, 8, 128), vmem(3, 2, 8, 128), vmem(3, 2, 8, 128),
-            dma(8), dma(8), dma(chunks), dma(chunks),
+            dma(8), dma(8), dma(chunks), dma(chunks), dma(2, chunks), dma(2, chunks),
             dma(steps, chunks), dma(steps, chunks), dma(steps, chunks), dma(steps, chunks),
         ],
         compiler_params=pltpu.CompilerParams(collective_id=0, has_side_effects=True, vmem_limit_bytes=56 * 2**20),

time: 24.2 us -> 23 us (0.950)
  Pallas kernels: 23.4 us -> 22.2 us
    pallas_call x1, Pallas kernels: 23.4 us -> 22.2 us  [body(): pl.pallas_call(functools.partial(kernel, bands, sectors, chunks), out_sha...]
where the time goes in v7:
time: 23 us; the launch traced here: 22.8 us
  Pallas kernels  22.2 us (97%)
  local copies, waits for them, and re-layouts  0.64 us (3%)
    pallas_call x1, Pallas kernels, body(): pl.pallas_call(functools.partial(kernel, bands, sectors, chunks), out_sha...  22.2 us
    unnamed x1, local copies, waits for them, and re-layouts  0.64 us

profile of v7, /device:TPU:0, one launch (start us, length us, event | category | flops | bytes accessed | tf_op | source)
XLA Modules:
  0.0 22.8 jit_solution(11122774374290812697)
XLA Ops:
  0.0 22.2 %disc_step.1 = f32[3,64,128]{2,1,0:T(8,128)S(1)} custom-call(f32[3,64,128]{2,1,0:T(8,128)} %bitcast.3, f32[8,128]{1,0:T(8,128)} %viscosity_in.1, f32[32]{0:T(128)} %rotation_in.1, s32[1,32]{1,0:T(1,128)} %shifts_in.1), custom_call_target="tpu_custom_call" | custom-call | tf_op jit(solution)/shard_map/disc_step/pallas_call | solution.py:333
  22.2 0.6 %copy.6 = f32[3,8,8,128]{3,2,1,0:T(8,128)} copy(f32[3,8,8,128]{3,2,1,0:T(8,128)S(1)} %bitcast.2) | data formatting | bytes 196608

commit v8 on v7

--- a/solution.py
+++ b/solution.py
@@ -11,6 +11,10 @@
 time_step = 0.3
 MESH = pl.DeviceIdType.MESH
 DEPTH = 3
+
+
+def bounds_of(radii):
+    return [0, radii // 4, radii * 5 // 8, radii * 7 // 8, radii]
 
 
 def neighbour_rates(centre, north, south, viscosity, spin):
@@ -181,14 +185,14 @@
 
     lax.fori_loop(2, radii + 2 * DEPTH - 2, second_row, 0, unroll=True)
 
-    per = radii // chunks
+    starts = bounds_of(radii)
 
     def final_row(c, r):
         i = r + DEPTH
         inside, spin, thick = row_facts(i)
         centre = second[i]
         rate = neighbour_rates(centre, second[i + 1], second[i - 1], thick, spin)
-        raws[c][place, r - c * per] = own[i, 0:3] / 3.0 + 2.0 / 3.0 * (centre + time_step * rate)[..., :128]
+        raws[c][place, r - starts[c]] = own[i, 0:3] / 3.0 + 2.0 / 3.0 * (centre + time_step * rate)[..., :128]
 
     def line_copy(to_right, d, c):
         held = raws[c].at[place]
@@ -218,7 +222,7 @@
                     line_copy(to_right, d, c).wait_recv()
 
     for c in range(chunks):
-        for r in range(c * per, (c + 1) * per):
+        for r in range(starts[c], starts[c + 1]):
             final_row(c, r)
         send(c)
 
@@ -234,7 +238,7 @@
 
     def picked(c, r, target):
         low_from, high_from, _ = sources(r, target)
-        return jnp.where(half, raws[c][low_from // 2, r - c * per], raws[c][high_from // 2, r - c * per])
+        return jnp.where(half, raws[c][low_from // 2, r - starts[c]], raws[c][high_from // 2, r - starts[c]])
 
     inner = jnp.logical_and(place >= 1, place <= places - 2)
     outer = jnp.logical_not(inner)
@@ -244,12 +248,12 @@
     end_mate = end + 1 - 2 * parity
 
     def mate_copy(c):
-        return remote(staged.at[0, c], gots[c].at[parity], mate_sent.at[c], mate_got.at[c], (band, mate))
+        return remote(staged[c].at[0], gots[c].at[parity], mate_sent.at[c], mate_got.at[c], (band, mate))
 
     def end_copy(other, c):
         target = lax.rem((end_mate if other else end) + sectors, sectors)
         return remote(
-            staged.at[1 + other, c], gots[c].at[parity], end_sent.at[other, c], end_got.at[parity, c], (band, target)
+            staged[c].at[1 + other], gots[c].at[parity], end_sent.at[other, c], end_got.at[parity, c], (band, target)
         )
 
     def from_helper(q, c):
@@ -257,22 +261,22 @@
 
     for c in range(chunks):
         get(c)
-        rows = range(c * per, (c + 1) * per)
+        rows = range(starts[c], starts[c + 1])
 
         @pl.when(beside)
         def _():
             for other, target in ((0, end), (1, end_mate)):
                 for r in rows:
-                    staged[1 + other, c, r - c * per] = picked(c, r, target)
+                    staged[c][1 + other, r - starts[c]] = picked(c, r, target)
                 end_copy(other, c).start()
 
         @pl.when(inner)
         def _():
             for r in rows:
-                staged[0, c, r - c * per] = picked(c, r, mate)
+                staged[c][0, r - starts[c]] = picked(c, r, mate)
             mate_copy(c).start()
             for r in rows:
-                gots[c][parity, r - c * per] = picked(c, r, sector)
+                gots[c][parity, r - starts[c]] = picked(c, r, sector)
 
     for c in range(chunks):
         @pl.when(inner)
@@ -284,9 +288,9 @@
             for q in range(2):
                 from_helper(q, c).wait_recv()
 
-        for r in range(c * per, (c + 1) * per):
+        for r in range(starts[c], starts[c + 1]):
             low_from, high_from, odd = sources(r, sector)
-            moved = jnp.where(half, gots[c][low_from % 2, r - c * per], gots[c][high_from % 2, r - c * per])
+            moved = jnp.where(half, gots[c][low_from % 2, r - starts[c]], gots[c][high_from % 2, r - starts[c]])
             moved = jnp.where(odd, pltpu.roll(moved, BLOCK, axis=2), moved)
             for f in range(3):
                 out[f, pl.ds(r, 8, stride=8), :] = moved[f]
@@ -325,7 +329,10 @@
 def body(fields, viscosity, rotation, shift_blocks):
     bands, sectors = lax.axis_size("rad"), lax.axis_size("azi")
     kinds, height, radii, width = fields.shape
-    places, chunks = sectors // 2, 4
+    places = sectors // 2
+    starts = bounds_of(radii)
+    chunks = len(starts) - 1
+    sizes = [starts[c + 1] - starts[c] for c in range(chunks)]
     rows = radii + 2 * DEPTH
     steps = places - 1
     vmem = lambda *shape: pltpu.VMEM(shape, jnp.float32)
@@ -340,9 +347,9 @@
             pltpu.SMEM(rotation.shape, jnp.float32), pltpu.SMEM(shift_blocks.shape, jnp.int32), dma(4),
             vmem(rows, 4, 8, 128), vmem(rows, 4, 8, 128),
             vmem(rows, 3, 8, 256), vmem(rows, 3, 8, 256),
-            [vmem(places, radii // chunks, 3, 8, 128) for _ in range(chunks)],
-            [vmem(2, radii // chunks, 3, 8, 128) for _ in range(chunks)],
-            vmem(3, chunks, radii // chunks, 3, 8, 128),
+            [vmem(places, size, 3, 8, 128) for size in sizes],
+            [vmem(2, size, 3, 8, 128) for size in sizes],
+            [vmem(3, size, 3, 8, 128) for size in sizes],
             vmem(2, 8, 128), vmem(3, 2, 8, 128), vmem(3, 2, 8, 128),
             dma(8), dma(8), dma(chunks), dma(chunks), dma(2, chunks), dma(2, chunks),
             dma(steps, chunks), dma(steps, chunks), dma(steps, chunks), dma(steps, chunks),

time: 23 us -> 23 us (level)
  no operation moved by 1% of the time
where the time goes in v8:
time: 23 us; the launch traced here: 22.9 us
  Pallas kernels  22.2 us (97%)
  local copies, waits for them, and re-layouts  0.64 us (3%)
    pallas_call x1, Pallas kernels, body(): pl.pallas_call(functools.partial(kernel, bands, sectors, chunks), out_sha...  22.2 us
    unnamed x1, local copies, waits for them, and re-layouts  0.64 us

profile of v8, /device:TPU:0, one launch (start us, length us, event | category | flops | bytes accessed | tf_op | source)
XLA Modules:
  0.0 22.9 jit_solution(920072123821393952)
XLA Ops:
  0.0 22.2 %disc_step.1 = f32[3,64,128]{2,1,0:T(8,128)S(1)} custom-call(f32[3,64,128]{2,1,0:T(8,128)} %bitcast.3, f32[8,128]{1,0:T(8,128)} %viscosity_in.1, f32[32]{0:T(128)} %rotation_in.1, s32[1,32]{1,0:T(1,128)} %shifts_in.1), custom_call_target="tpu_custom_call" | custom-call | tf_op jit(solution)/shard_map/disc_step/pallas_call | solution.py:340
  22.2 0.6 %copy.6 = f32[3,8,8,128]{3,2,1,0:T(8,128)} copy(f32[3,8,8,128]{3,2,1,0:T(8,128)S(1)} %bitcast.2) | data formatting | bytes 196608

commit v9 on v8

--- a/solution.py
+++ b/solution.py
@@ -14,7 +14,7 @@
 
 
 def bounds_of(radii):
-    return [0, radii // 4, radii * 5 // 8, radii * 7 // 8, radii]
+    return [0, radii // 2, radii]
 
 
 def neighbour_rates(centre, north, south, viscosity, spin):

time: 23 us -> 22.8 us (level)
    pallas_call x1, Pallas kernels: 22.2 us -> 22 us  [body(): pl.pallas_call(functools.partial(kernel, bands, sectors, chunks), out_sha...]
where the time goes in v9:
time: 22.8 us; the launch traced here: 22.6 us
  Pallas kernels  22 us (96%)
  local copies, waits for them, and re-layouts  0.64 us (3%)
    pallas_call x1, Pallas kernels, body(): pl.pallas_call(functools.partial(kernel, bands, sectors, chunks), out_sha...  22 us
    unnamed x1, local copies, waits for them, and re-layouts  0.64 us

profile of v9, /device:TPU:0, one launch (start us, length us, event | category | flops | bytes accessed | tf_op | source)
XLA Modules:
  0.0 22.6 jit_solution(18116177782318156108)
XLA Ops:
  0.0 22.0 %disc_step.1 = f32[3,64,128]{2,1,0:T(8,128)S(1)} custom-call(f32[3,64,128]{2,1,0:T(8,128)} %bitcast.3, f32[8,128]{1,0:T(8,128)} %viscosity_in.1, f32[32]{0:T(128)} %rotation_in.1, s32[1,32]{1,0:T(1,128)} %shifts_in.1), custom_call_target="tpu_custom_call" | custom-call | tf_op jit(solution)/shard_map/disc_step/pallas_call | solution.py:340
  22.0 0.6 %copy.6 = f32[3,8,8,128]{3,2,1,0:T(8,128)} copy(f32[3,8,8,128]{3,2,1,0:T(8,128)S(1)} %bitcast.2) | data formatting | bytes 196608

commit v10 on v9

--- a/solution.py
+++ b/solution.py
@@ -14,7 +14,7 @@
 
 
 def bounds_of(radii):
-    return [0, radii // 2, radii]
+    return [radii * c // 4 for c in range(5)]
 
 
 def neighbour_rates(centre, north, south, viscosity, spin):
@@ -147,16 +147,17 @@
         own[0:DEPTH] = jnp.zeros((DEPTH, 4, 8, 128), jnp.float32)
         side[0:DEPTH] = jnp.zeros((DEPTH, 4, 8, 128), jnp.float32)
 
-    @pl.when(has_up)
-    def _():
-        for copy in down:
-            copy.wait_recv()
-        unpack(2, 0, range(0, DEPTH), last)
-
-    @pl.when(jnp.logical_not(has_up))
-    def _():
-        own[last:last + DEPTH] = jnp.zeros((DEPTH, 4, 8, 128), jnp.float32)
-        side[last:last + DEPTH] = jnp.zeros((DEPTH, 4, 8, 128), jnp.float32)
+    def take_upper_halo():
+        @pl.when(has_up)
+        def _():
+            for copy in down:
+                copy.wait_recv()
+            unpack(2, 0, range(0, DEPTH), last)
+
+        @pl.when(jnp.logical_not(has_up))
+        def _():
+            own[last:last + DEPTH] = jnp.zeros((DEPTH, 4, 8, 128), jnp.float32)
+            side[last:last + DEPTH] = jnp.zeros((DEPTH, 4, 8, 128), jnp.float32)
 
     def start_row(i):
         return jnp.concatenate([own[i, 0:3], side[i, 0:3]], axis=2)
@@ -174,8 +175,6 @@
         first[i] = jnp.where(inside, centre + time_step * rate, 0.0)
         return 0
 
-    lax.fori_loop(1, radii + 2 * DEPTH - 1, first_row, 0, unroll=True)
-
     def second_row(i, _):
         inside, spin, thick = row_facts(i)
         centre = first[i]
@@ -183,8 +182,6 @@
         second[i] = jnp.where(inside, 0.75 * start_row(i) + 0.25 * (centre + time_step * rate), 0.0)
         return 0
 
-    lax.fori_loop(2, radii + 2 * DEPTH - 2, second_row, 0, unroll=True)
-
     starts = bounds_of(radii)
 
     def final_row(c, r):
@@ -221,7 +218,15 @@
                 def _():
                     line_copy(to_right, d, c).wait_recv()
 
+    first_end, second_end = 1, 2
     for c in range(chunks):
+        need_first = min(starts[c + 1] + DEPTH + 2, last + DEPTH - 1)
+        need_second = min(starts[c + 1] + DEPTH + 1, last + DEPTH - 2)
+        if first_end < last <= need_first:
+            take_upper_halo()
+        lax.fori_loop(first_end, need_first, first_row, 0, unroll=True)
+        lax.fori_loop(second_end, need_second, second_row, 0, unroll=True)
+        first_end, second_end = need_first, need_second
         for r in range(starts[c], starts[c + 1]):
             final_row(c, r)
         send(c)

time: 22.8 us -> 22.6 us (level)
  no operation moved by 1% of the time
where the time goes in v10:
time: 22.6 us; the launch traced here: 22.4 us
  Pallas kernels  21.8 us (96%)
  local copies, waits for them, and re-layouts  0.64 us (3%)
    pallas_call x1, Pallas kernels, body(): pl.pallas_call(functools.partial(kernel, bands, sectors, chunks), out_sha...  21.8 us
    unnamed x1, local copies, waits for them, and re-layouts  0.64 us

profile of v10, /device:TPU:0, one launch (start us, length us, event | category | flops | bytes accessed | tf_op | source)
XLA Modules:
  0.0 22.4 jit_solution(17715403201802306643)
XLA Ops:
  0.0 21.8 %disc_step.1 = f32[3,64,128]{2,1,0:T(8,128)S(1)} custom-call(f32[3,64,128]{2,1,0:T(8,128)} %bitcast.3, f32[8,128]{1,0:T(8,128)} %viscosity_in.1, f32[32]{0:T(128)} %rotation_in.1, s32[1,32]{1,0:T(1,128)} %shifts_in.1), custom_call_target="tpu_custom_call" | custom-call | tf_op jit(solution)/shard_map/disc_step/pallas_call | solution.py:345
  21.8 0.6 %copy.6 = f32[3,8,8,128]{3,2,1,0:T(8,128)} copy(f32[3,8,8,128]{3,2,1,0:T(8,128)S(1)} %bitcast.2) | data formatting | bytes 196608

commit v11 on v10

--- a/solution.py
+++ b/solution.py
@@ -14,7 +14,7 @@
 
 
 def bounds_of(radii):
-    return [radii * c // 4 for c in range(5)]
+    return [0, radii // 2, radii]
 
 
 def neighbour_rates(centre, north, south, viscosity, spin):

time: 22.6 us -> 22.6 us (level)
  no operation moved by 1% of the time
where the time goes in v11:
time: 22.6 us; the launch traced here: 22.4 us
  Pallas kernels  21.8 us (96%)
  local copies, waits for them, and re-layouts  0.64 us (3%)
    pallas_call x1, Pallas kernels, body(): pl.pallas_call(functools.partial(kernel, bands, sectors, chunks), out_sha...  21.8 us
    unnamed x1, local copies, waits for them, and re-layouts  0.64 us

profile of v11, /device:TPU:0, one launch (start us, length us, event | category | flops | bytes accessed | tf_op | source)
XLA Modules:
  0.0 22.4 jit_solution(3346450333063964824)
XLA Ops:
  0.0 21.8 %disc_step.1 = f32[3,64,128]{2,1,0:T(8,128)S(1)} custom-call(f32[3,64,128]{2,1,0:T(8,128)} %bitcast.3, f32[8,128]{1,0:T(8,128)} %viscosity_in.1, f32[32]{0:T(128)} %rotation_in.1, s32[1,32]{1,0:T(1,128)} %shifts_in.1), custom_call_target="tpu_custom_call" | custom-call | tf_op jit(solution)/shard_map/disc_step/pallas_call | solution.py:345
  21.8 0.6 %copy.6 = f32[3,8,8,128]{3,2,1,0:T(8,128)} copy(f32[3,8,8,128]{3,2,1,0:T(8,128)S(1)} %bitcast.2) | data formatting | bytes 196608
